TPU v7x, 256 devices: a whole 4x4x8 slice. The times are simulated.
256 devices in a mesh: rep: 8 (over y_lo, x), fsdp: 32 (over z, y_hi, core).
Axes of the slice: x: 4, y: 4 (y_hi: 2, y_lo: 2; y = y_hi * 2 + y_lo), z: 8, core: 2. Of those that a mesh axis runs over, the one named last changes fastest.
Arguments:
- hidden_states: bfloat16 [65536, 8192], P(('rep', 'fsdp')), may hold values from -6 to 6
- queries: bfloat16 [65536, 4096], P(('rep', 'fsdp')), may hold values from -170 to 170
- token_ids: int32 [65536], P(('rep', 'fsdp')), may hold values from 0 to 128000, as said below
- local_weights: bfloat16 [8, 8192, 1024], P('rep', 'fsdp'), may hold values from -0.0625 to 0.0625
- outer_base: float32 [8192, 1024], P('fsdp'), may hold values from -1 to 1
- momentum: float32 [8192, 1024], P('fsdp'), may hold values from -0.08 to 0.08
- outer_rates: float32 [8], replicated, may hold values from 0.2 to 1
- frag_index: int32 [1], replicated, may hold values from 0 to 7
Outputs:
- context: bfloat16 [65536, 4096], P(('rep', 'fsdp'))
- new_base: float32 [8192, 1024], P('fsdp')
- new_momentum: float32 [8192, 1024], P('fsdp')
Inputs may be any that keep to these rules, and one draw needn't show every extreme that they name: `token_ids`: each device's first token, at a multiple of 256, has id 128000; ids below 128000 are ordinary tokens.
All inputs are finite; a program needn't handle non-finite values.
Results may differ from a plain program's by a relative error of at most 0.006.
Values may be sent and summed in bfloat16 or wider, within the bound.
No kernel may reach another device: no remote copies, remote signals or barrier semaphores. Data moves between devices by JAX's collectives and lax.ppermute only.
A program may use at most 128 MiB of HBM per device.

v0:
```python
import math

import jax
import jax.numpy as jnp
import numpy as np
from jax import lax
from jax.sharding import PartitionSpec as P

HEAD = 128
BLOCK = 32
BOS = 128000


rope_base = 500000.0
momentum_coef = 0.9


def rotate(head_vals, positions):
    half_dim = head_vals.shape[-1] // 2
    steps_idx = jnp.arange(half_dim, dtype=jnp.float32)
    inverse = rope_base ** (-2.0 * steps_idx / head_vals.shape[-1])
    angles = positions[:, None] * inverse[None, :]
    cosine = jnp.cos(angles)[:, None, :]
    sine_part = jnp.sin(angles)[:, None, :]
    first_half = head_vals[..., :half_dim]
    second_half = head_vals[..., half_dim:]
    return jnp.concatenate(
        [
            first_half * cosine - second_half * sine_part,
            second_half * cosine + first_half * sine_part,
        ],
        axis=-1,
    )


def layout(token_row):
    token_count = token_row.shape[0]
    starts = token_row == BOS
    position_idx = jnp.arange(token_count, dtype=jnp.int32)
    latest = lax.cummax(jnp.where(starts, position_idx, 0), axis=0)
    positions = (position_idx - latest).astype(jnp.float32)
    documents = jnp.cumsum(starts.astype(jnp.int32))
    allowed = (documents[:, None] == documents[None, :]) & (
        position_idx[None, :] <= position_idx[:, None]
    )
    return (positions, allowed)


def attend(kv_rows, query_rows, token_row):
    positions, allowed = layout(token_row)
    token_count = query_rows.shape[0]
    kv_heads = kv_rows.shape[1] // (2 * HEAD)
    query_heads = query_rows.shape[1] // HEAD
    key_rows = rotate(
        kv_rows[:, : kv_heads * HEAD].reshape(token_count, kv_heads, HEAD), positions
    ).astype(jnp.bfloat16)
    value_rows = (
        kv_rows[:, kv_heads * HEAD :].reshape(token_count, kv_heads, HEAD).astype(jnp.bfloat16)
    )
    rotated = rotate(
        query_rows.astype(jnp.float32).reshape(token_count, query_heads, HEAD), positions
    ).astype(jnp.bfloat16)
    grouped = rotated.reshape(token_count, kv_heads, query_heads // kv_heads, HEAD)
    scores = jnp.einsum(
        "tkgd,skd->kgts", grouped, key_rows, preferred_element_type=jnp.float32
    ) / math.sqrt(HEAD)
    scores = jnp.where(allowed[None, None], scores, -1e30)
    row_peak = jnp.max(scores, axis=-1, keepdims=True)
    exponent = jnp.exp(scores - row_peak)
    weights = (exponent / jnp.sum(exponent, axis=-1, keepdims=True)).astype(jnp.bfloat16)
    context = jnp.einsum("kgts,skd->tkgd", weights, value_rows, preferred_element_type=jnp.float32)
    return context.reshape(token_count, query_heads * HEAD).astype(jnp.bfloat16)


def encode(delta):
    shard_rows = delta.shape[0]
    blocks = delta.reshape(shard_rows, delta.shape[1] // BLOCK, BLOCK)
    block_peak = jnp.max(jnp.abs(blocks), axis=-1)
    block_exp = jnp.full(block_peak.shape, -30, jnp.int32)
    for level in range(-29, 3):
        block_exp = block_exp + (block_peak >= np.float32(2.0**level)).astype(jnp.int32)
    block_scale = jnp.zeros(block_peak.shape, jnp.float32)
    block_inverse = jnp.zeros(block_peak.shape, jnp.float32)
    for level in range(-30, 3):
        chosen = block_exp == level
        block_scale = jnp.where(chosen, np.float32(2.0 ** (level - 8)), block_scale)
        block_inverse = jnp.where(chosen, np.float32(2.0 ** (8 - level)), block_inverse)
    scaled = blocks * block_inverse[..., None]
    magnitude = jnp.abs(scaled)
    element_exp = jnp.full(magnitude.shape, -6, jnp.int32)
    for level in range(-5, 9):
        element_exp = element_exp + (magnitude >= np.float32(2.0**level)).astype(jnp.int32)
    step_size = jnp.zeros(magnitude.shape, jnp.float32)
    step_inverse = jnp.zeros(magnitude.shape, jnp.float32)
    for level in range(-6, 9):
        chosen = element_exp == level
        step_size = jnp.where(chosen, np.float32(2.0 ** (level - 3)), step_size)
        step_inverse = jnp.where(chosen, np.float32(2.0 ** (3 - level)), step_inverse)
    counted = jnp.floor(magnitude * step_inverse + 0.5)
    coded_vals = jnp.sign(scaled) * jnp.minimum(counted * step_size, 448.0)
    return (coded_vals.astype(jnp.bfloat16), block_scale.astype(jnp.bfloat16))


def outer_step(total, base_rows, moment_rows, rate, groups):
    outer_grad = total / groups
    moment_next = momentum_coef * moment_rows + outer_grad
    base_next = base_rows - rate * (outer_grad + momentum_coef * moment_next)
    return (base_next, moment_next)


def body(
    hidden_states, queries, token_ids, local_weights, outer_base, momentum, outer_rates, frag_index
):
    own_weights = local_weights[0]
    kv_rows = jnp.dot(
        hidden_states,
        lax.all_gather(own_weights, "fsdp", axis=0, tiled=True),
        preferred_element_type=jnp.float32,
    )
    context = attend(kv_rows, queries, token_ids)
    groups = lax.axis_size("rep")
    shard_rows = outer_base.shape[0]
    delta = outer_base - own_weights.astype(jnp.float32)
    codes, scales = encode(delta)
    table = jnp.arange(outer_rates.shape[0], dtype=jnp.int32)
    rate = jnp.sum(jnp.where(table == frag_index[0], outer_rates, 0.0))
    all_codes, all_scales = (
        lax.all_gather(codes[None], "rep", axis=0, tiled=True),
        lax.all_gather(scales[None], "rep", axis=0, tiled=True),
    )
    total = jnp.sum(
        all_codes.astype(jnp.float32) * all_scales.astype(jnp.float32)[..., None], axis=0
    ).reshape(shard_rows, own_weights.shape[1])
    new_base, new_momentum = outer_step(total, outer_base, momentum, rate, groups)
    return (context, new_base, new_momentum)


def solution(mesh):
    placed = (
        P(("rep", "fsdp"), None),
        P(("rep", "fsdp"), None),
        P(("rep", "fsdp")),
        P("rep", "fsdp", None),
        P("fsdp", None),
        P("fsdp", None),
        P(),
        P(),
    )
    return jax.shard_map(
        body,
        mesh=mesh,
        in_specs=placed,
        out_specs=(P(("rep", "fsdp"), None), P("fsdp", None), P("fsdp", None)),
        check_vma=False,
    )
```

profile of v0, /device:TPU:1, one launch (start us, length us, event | category | flops | bytes accessed | tf_op | source)
XLA Modules:
  0.0 243.3 jit_solution(16785383638732944500)
XLA Ops:
  7.2 1.7 copy.40
  8.9 2.0 copy.37
  11.0 1.3 bitcast_reduce_fusion
  12.7 4.2 %multiply_convert_fusion = bf16[1,256,32,32]{1,3,2,0:T(8,128)(2,1)} fusion(f32[1,256,32,32]{1,3,2,0:T(8,128)S(1)} %bitcast.219, f32[256,32]{0,1:T(8,128)S(1)} %select_select_fusion), kind=kLoop, calls=%fused_computation.26 | loop fusion | flops 25427968 | bytes 1605632 | tf_op jit(solution)/shard_map/convert_element_type | solution.py:101
  17.0 0.7 all-gather.6.cloned.1.call-update
  18.2 2.7 %copy.52 = f32[32,8,32,128]{3,2,1,0:T(8,128)} copy(f32[32,8,32,128]{3,1,2,0:T(8,128)S(1)} %convert_bitcast_fusion) | data formatting | bytes 8388608
  21.8 24.9 %all_gather.11 = bf16[8,256,32]{1,2,0:T(8,128)(2,1)S(1)} all-gather(bf16[1,256,32]{1,2,0:T(8,128)(2,1)S(1)} %get-tuple-element.12), channel_id=1, replica_groups=mesh['rep'=8,'fsdp'=32] {'rep'}, dimensions={0}, use_global_device_ids=true | all-gather | bytes 147456 | tf_op jit(solution)/shard_map/all_gather | solution.py:129
  46.6 0.7 convert_element_type.913
  47.4 1.3 copy.39
  51.0 5.0 %fusion.44 = (f32[256,32,64]{2,1,0:T(8,128)S(1)}, f32[256,32,64]{2,1,0:T(8,128)S(1)}) fusion(f32[256,32,128]{2,1,0:T(8,128)} %bitcast.216), kind=kLoop, calls=%fused_computation.134 | loop fusion | bytes 8388608 | tf_op jit(solution)/shard_map/slice | solution.py:25
  56.0 6.2 %subtract_convert_fusion = (bf16[256,32,64]{2,0,1:T(8,128)(2,1)S(1)}, bf16[256,32,64]{2,0,1:T(8,128)(2,1)}) fusion(f32[256,32,64]{2,1,0:T(8,128)S(1)} %get-tuple-element.37, f32[256,32,64]{2,1,0:T(8,128)S(1)} %get-tuple-element.36, f32[256,64]{1,0:T(8,128)S(1)} %get-tuple-element.45, f32[256,64]{1,0:T(8,128)S(1)} %get-tuple-element.44), kind=kLoop, calls=%fused_computation.12 | loop fusion | flops 4194304 | bytes 6422528 | tf_op jit(solution)/shard_map/convert.35
  62.2 14.6 %all-gather.4.cloned.1.call-done = bf16[8,256,32,32]{1,3,2,0:T(8,128)(2,1)} async-done(((bf16[1,256,32,32]{1,3,2,0:T(8,128)(2,1)}), bf16[8,256,32,32]{1,3,2,0:T(8,128)(2,1)}) %all-gather.4.cloned.1.call-update) | async-done | bytes 4194320 | tf_op jit(solution)/shard_map/all_gather | solution.py:128
  76.8 3.5 %multiply_reduce_fusion = f32[256,32,32]{0,2,1:T(8,128)S(1)} fusion(bf16[8,256,32,32]{1,3,2,0:T(8,128)(2,1)} %all-gather.4.cloned.1.call-done, f32[8,256,32]{1,2,0:T(8,128)} %convert_element_type.913), kind=kLoop, calls=%fused_computation.4 | loop fusion | flops 6029312 | bytes 5505024 | tf_op jit(solution)/shard_map/reduce_sum | solution.py:131
  80.4 2.2 bitcast_add_fusion.1
  82.6 2.5 %copy.42 = f32[256,1024]{1,0:T(8,128)} copy(f32[256,1024]{0,1:T(8,128)} %get-tuple-element.39) | data formatting | bytes 2097152
  85.1 2.5 %copy.43 = f32[256,1024]{1,0:T(8,128)} copy(f32[256,1024]{0,1:T(8,128)} %get-tuple-element.38) | data formatting | bytes 2097152
  87.6 129.0 %all-gather.6.cloned.1.call-done = bf16[1,8192,1024]{2,1,0:T(8,128)(2,1)} async-done(((bf16[1,256,1024]{2,1,0:T(8,128)(2,1)}), bf16[1,8192,1024]{2,1,0:T(8,128)(2,1)}) %all-gather.6.cloned.1.call-update) | async-done | bytes 16777232 | tf_op jit(solution)/shard_map/all_gather | solution.py:117
  216.6 9.5 %fusion.1 = f32[256,1024]{1,0:T(8,128)S(1)} fusion(bf16[256,8192]{1,0:T(8,128)(2,1)} %param.8, bf16[1,8192,1024]{2,1,0:T(8,128)(2,1)} %all-gather.6.cloned.1.call-done), kind=kOutput, calls=%fused_computation.1 | convolution fusion | flops 4294967296 | bytes 22020096 | tf_op jit(solution)/shard_map/dot_general | solution.py:115
  226.2 0.8 copy.47
  227.7 1.1 copy-done
  228.8 1.6 fusion.8
  230.4 2.4 fusion.46
  232.7 0.8 fusion.12
  233.6 2.9 %copy.41 = bf16[256,4096]{1,0:T(8,128)(2,1)} copy(bf16[256,4096]{0,1:T(8,128)(2,1)S(1)} %bitcast.220) | data formatting | bytes 4194304
  (41 shorter events, 4.3 us)
Async XLA Ops:
  7.2 10.5 %copy-start.2 = (bf16[256,4096]{1,0:T(8,128)(2,1)S(1)}, bf16[256,4096]{1,0:T(8,128)(2,1)}, u32[]{:S(2)}) copy-start(bf16[256,4096]{1,0:T(8,128)(2,1)} %param.9) | copy-start | bytes 6291460
  7.2 69.6 %all-gather.4.cloned.1.call-start = ((), (), s32[]{:S(2)}) async-start(), calls=%async_computation | async-start | bytes 4718592 | tf_op jit(solution)/shard_map/all_gather | solution.py:128
  16.9 199.7 %all-gather.6.cloned.1.call-start = ((), (), s32[]{:S(2)}) async-start(), calls=%async_computation.1 | async-start | bytes 17301504 | tf_op jit(solution)/shard_map/all_gather | solution.py:117
  18.2 2.7 %copy-start.5 = (s32[256]{0:T(256)S(1)}, s32[256]{0:T(256)}, u32[]{:S(2)}) copy-start(s32[256]{0:T(256)} %param.10) | copy-start | bytes 3076
  18.2 29.2 %copy-start.3 = (f32[256,1024]{1,0:T(8,128)S(1)}, f32[256,1024]{1,0:T(8,128)}, u32[]{:S(2)}) copy-start(f32[256,1024]{1,0:T(8,128)} %param.13) | copy-start | bytes 3145732
  18.2 31.4 %copy-start.6 = (f32[8]{0:T(128)S(1)}, f32[8]{0:T(128)}, u32[]{:S(2)}) copy-start(f32[8]{0:T(128)} %param.14) | copy-start | bytes 100
  76.8 3.6 %copy-start.1 = (f32[256,1024]{0,1:T(8,128)S(1)}, f32[256,1024]{0,1:T(8,128)}, u32[]{:S(2)}) copy-start(f32[256,1024]{0,1:T(8,128)} %copy.39) | copy-start | bytes 3145732
  227.2 1.6 copy-start
  230.3 2.4 copy-start.4
Sparse Core Ops, SparseCore 0:
  17.0 59.6 all-gather.3
  79.6 136.9 all-gather.5
where the time goes:
time: 244 us; the launch traced here: 243 us
  waiting for transfers between devices  144 us (59%)
  blocking collectives  24.9 us (10%)
  other arithmetic  23.7 us (10%)
  local copies, waits for them, and re-layouts  23.6 us (10%)
  between operations  14.9 us (6%)
  matrix products  11.8 us (5%)
    all_gather x1, waiting for transfers between devices, body(): lax.all_gather(own_weights, 'fsdp', axis=0, tiled=True)  129 us
    all_gather x1, blocking collectives, body(): lax.all_gather(scales[None], 'rep', axis=0, tiled=True)  24.9 us
    unnamed x21, local copies, waits for them, and re-layouts  16.8 us
    all_gather x1, waiting for transfers between devices, body(): lax.all_gather(codes[None], 'rep', axis=0, tiled=True)  14.6 us
    dot_general x1, matrix products, body(): jnp.dot(hidden_states, lax.all_gather(own_weights, 'fsdp', axis=0, tiled=...  9.49 us
    another operation x9, other arithmetic  7.13 us
    slice x2, local copies, waits for them, and re-layouts, rotate(): first_half = head_vals[..., :half_dim]  5.33 us
  transfers between devices with their start and end apart: 2, of which 2 were waited for; matrix products, arithmetic and copies ran while one was open for 12% of the time, Pallas kernels for 0%

commit v1 on v0

v1 whole, which is shorter than its diff:
```python
import functools
import math

import jax
import jax.numpy as jnp
from jax import lax
from jax.experimental import pallas as pl
from jax.experimental.pallas import tpu as pltpu
from jax.sharding import PartitionSpec as P

HEAD = 128
BLOCK = 32
BOS = 128000
TOK = 256
ROWS = 256
KV_HEADS = 4
HALF = KV_HEADS * HEAD
GROUP_HEADS = 8
Z, Y_HI, CORES = 8, 2, 2
X = 4

rope_base = 500000.0
momentum_coef = 0.9
F32 = jnp.float32
BF16 = jnp.bfloat16


def fsdp_pairs(move):
    pairs = []
    for z in range(Z):
        for y in range(Y_HI):
            for c in range(CORES):
                z2, y2, c2 = move(z, y, c)
                pairs.append(
                    (
                        (z * Y_HI + y) * CORES + c,
                        ((z2 % Z) * Y_HI + y2 % Y_HI) * CORES + c2 % CORES,
                    )
                )
    return pairs


UP = fsdp_pairs(lambda z, y, c: (z + 1, y, c))
DOWN = fsdp_pairs(lambda z, y, c: (z - 1, y, c))
ACROSS = fsdp_pairs(lambda z, y, c: (z, y + 1, c))
SWAP = fsdp_pairs(lambda z, y, c: (z, y, c + 1))


def send(block, pairs):
    return lax.ppermute(block, "fsdp", pairs)


def tie(*arrays):
    return lax.optimization_barrier(arrays)


def pick_kernel(core_ref, hidden_ref, out_ref):
    out_ref[...] = hidden_ref[...]


def pick_columns(hidden, core):
    blocks = Z * Y_HI
    return pl.pallas_call(
        pick_kernel,
        out_shape=jax.ShapeDtypeStruct((TOK, blocks * ROWS), BF16),
        grid_spec=pltpu.PrefetchScalarGridSpec(
            num_scalar_prefetch=1,
            grid=(blocks,),
            in_specs=[pl.BlockSpec((TOK, ROWS), lambda i, core: (0, 2 * i + 1 - core[0]))],
            out_specs=pl.BlockSpec((TOK, ROWS), lambda i, core: (0, i)),
        ),
        cost_estimate=pl.CostEstimate(
            flops=0, bytes_accessed=4 * TOK * blocks * ROWS, transcendentals=0
        ),
    )(core, hidden)


def multiply_kernel(n_h, uses, index_ref, *refs):
    own, other = refs[:n_h], refs[n_h : 2 * n_h]
    n_w = len(uses)
    weights = refs[2 * n_h : 2 * n_h + n_w]
    rest = refs[2 * n_h + n_w :]
    totals, outs = (rest[:4], rest[4:]) if len(rest) == 8 else (None, rest)
    for side in range(2):
        states = (own, other)[side]
        for part in range(2):
            total = None if totals is None else totals[2 * side + part][...]
            for (cols, where), weight in zip(uses, weights):
                if where != part:
                    continue
                left = [states[k][...] for k in cols]
                left = left[0] if len(left) == 1 else jnp.concatenate(left, axis=1)
                term = jnp.dot(left, weight[...], preferred_element_type=F32)
                total = term if total is None else total + term
            outs[2 * side + part][...] = total


def multiply(hidden, hidden_other, pieces, core, totals):
    sources = []
    uses = []
    for blocks, part, _ in pieces:
        cols = []
        for block in blocks:
            known = [k for k, (name, _) in enumerate(sources) if name == block[0]]
            if known:
                cols.append(known[0])
            else:
                cols.append(len(sources))
                sources.append(block)
        uses.append((tuple(cols), part))
    n_h = len(sources)
    index = jnp.stack([s[1] for s in sources] + [core]).astype(jnp.int32)
    own_specs = [
        pl.BlockSpec(
            (TOK, ROWS), functools.partial(lambda k, i, at: (0, 2 * at[k] + at[n_h]), k)
        )
        for k in range(n_h)
    ]
    other_specs = [
        pl.BlockSpec((TOK, ROWS), functools.partial(lambda k, i, at: (0, at[k]), k))
        for k in range(n_h)
    ]
    weights = [p[2] for p in pieces]
    whole = pl.BlockSpec(memory_space=pltpu.VMEM)
    n_t = 0 if totals is None else 4
    depth = sum(w.shape[0] for w in weights)
    return pl.pallas_call(
        functools.partial(multiply_kernel, n_h, uses),
        out_shape=[jax.ShapeDtypeStruct((TOK, HALF), F32)] * 4,
        grid_spec=pltpu.PrefetchScalarGridSpec(
            num_scalar_prefetch=1,
            grid=(1,),
            in_specs=own_specs + other_specs + [whole] * (len(weights) + n_t),
            out_specs=[whole] * 4,
        ),
        input_output_aliases={1 + 2 * n_h + len(weights) + k: k for k in range(n_t)},
        cost_estimate=pl.CostEstimate(
            flops=4 * TOK * depth * HALF,
            bytes_accessed=2 * depth * HALF + 4 * TOK * depth,
            transcendentals=0,
        ),
        compiler_params=pltpu.CompilerParams(vmem_limit_bytes=20 * 2**20),
    )(
        index,
        *([hidden] * n_h),
        *([hidden_other] * n_h),
        *weights,
        *(totals or ()),
    )


def rope(head, cosine, sine):
    return head * cosine + pltpu.roll(head, HEAD // 2, 1) * sine


def rotate_kernel(query_ref, cos_ref, sin_ref, out_ref):
    for h in range(GROUP_HEADS):
        cols = slice(h * HEAD, (h + 1) * HEAD)
        out_ref[:, cols] = rope(
            query_ref[:, cols].astype(F32), cos_ref[...], sin_ref[...]
        ).astype(BF16)


def rotate_queries(queries, cosine, sine):
    width = GROUP_HEADS * HEAD
    spec = pl.BlockSpec((TOK, width), lambda h: (0, h))
    table = pl.BlockSpec((TOK, HEAD), lambda h: (0, 0))
    return pl.pallas_call(
        rotate_kernel,
        out_shape=jax.ShapeDtypeStruct(queries.shape, BF16),
        grid=(KV_HEADS,),
        in_specs=[spec, table, table],
        out_specs=spec,
        cost_estimate=pl.CostEstimate(
            flops=4 * queries.size, bytes_accessed=4 * queries.size, transcendentals=0
        ),
    )(queries, cosine, sine)


def attend_kernel(
    query_ref, key_ref, key_add_ref, val_ref, val_add_ref, cos_ref, sin_ref, bias_ref, out_ref
):
    keys = rope(key_ref[...] + key_add_ref[...], cos_ref[...], sin_ref[...]).astype(BF16)
    vals = (val_ref[...] + val_add_ref[...]).astype(BF16)
    vals = jnp.concatenate([vals, jnp.ones((TOK, HEAD), BF16)], axis=1)
    factor = math.log2(math.e) / math.sqrt(HEAD)
    part = TOK // 2
    for h in range(GROUP_HEADS):
        cols = slice(h * HEAD, (h + 1) * HEAD)
        for r in range(2):
            rows = slice(r * part, (r + 1) * part)
            seen = (r + 1) * part
            scores = lax.dot_general(
                query_ref[rows, cols],
                keys[:seen],
                (((1,), (1,)), ((), ())),
                preferred_element_type=F32,
            )
            scores = scores + bias_ref[rows, :seen]
            peak = jnp.max(scores, axis=1, keepdims=True)
            weights = jnp.exp2((scores - peak) * factor).astype(BF16)
            both = jnp.dot(weights, vals[:seen], preferred_element_type=F32)
            out_ref[rows, cols] = (both[:, :HEAD] / both[:, HEAD:]).astype(BF16)


def attend(rotated, keys, keys_add, vals, vals_add, cosine, sine, bias):
    width = GROUP_HEADS * HEAD
    wide = pl.BlockSpec((TOK, width), lambda h: (0, h))
    one = pl.BlockSpec((TOK, HEAD), lambda h: (0, h))
    table = pl.BlockSpec((TOK, HEAD), lambda h: (0, 0))
    square = pl.BlockSpec((TOK, TOK), lambda h: (0, 0))
    return pl.pallas_call(
        attend_kernel,
        out_shape=jax.ShapeDtypeStruct(rotated.shape, BF16),
        grid=(KV_HEADS,),
        in_specs=[wide, one, one, one, one, table, table, square],
        out_specs=wide,
        cost_estimate=pl.CostEstimate(
            flops=4 * rotated.size * TOK,
            bytes_accessed=4 * rotated.size,
            transcendentals=rotated.size * 2,
        ),
        compiler_params=pltpu.CompilerParams(vmem_limit_bytes=24 * 2**20),
    )(rotated, keys, keys_add, vals, vals_add, cosine, sine, bias)


def tables(token_row):
    token = jnp.arange(TOK, dtype=jnp.int32)
    started = (token_row == BOS)[None, :] & (token[None, :] <= token[:, None])
    latest = jnp.max(jnp.where(started, token[None, :], 0), axis=1)
    positions = (token - latest).astype(F32)
    steps = jnp.arange(HEAD // 2, dtype=F32)
    inverse = rope_base ** (-2.0 * steps / HEAD)
    angles = positions[:, None] * inverse[None, :]
    cosine, sine = jnp.cos(angles), jnp.sin(angles)
    allowed = (token[None, :] <= token[:, None]) & (token[None, :] >= latest[:, None])
    bias = jnp.where(allowed, 0.0, -1e30).astype(F32)
    return (
        jnp.concatenate([cosine, cosine], axis=1),
        jnp.concatenate([-sine, sine], axis=1),
        bias,
    )


def top_bit(number):
    return 31 - lax.clz(jnp.maximum(number, 1))


def power(exponent):
    return lax.shift_left(jnp.full(exponent.shape, 1, jnp.int32), exponent).astype(F32)


def encode_kernel(base_ref, weight_ref, out_ref):
    lanes = lax.broadcasted_iota(jnp.int32, (base_ref.shape[0], HEAD), 1)
    for j in range(base_ref.shape[1] // HEAD):
        cols = slice(j * HEAD, (j + 1) * HEAD)
        delta = base_ref[:, cols] - weight_ref[:, cols].astype(F32)
        size = jnp.abs(delta)
        peak = size
        for reach in (1, 2, 4, 8, 16):
            beside = jnp.where(
                (lanes & reach) != 0,
                pltpu.roll(peak, reach, 1),
                pltpu.roll(peak, HEAD - reach, 1),
            )
            peak = jnp.maximum(peak, beside)
        block = top_bit((peak * 2.0**30).astype(jnp.int32))
        scale = power(block) * 2.0**-38
        value = size * (power(30 - block) * 2.0**8)
        step = top_bit((value * 2.0**6).astype(jnp.int32))
        counted = jnp.floor(value * (power(14 - step) * 2.0**-5) + 0.5)
        code = jnp.minimum(counted * (power(step) * 2.0**-9), 448.0) * scale
        out_ref[:, cols] = jnp.where(delta < 0, -code, code).astype(BF16)


def encode(base, weights):
    rows, width = base.shape
    tall = rows // 2
    spec = pl.BlockSpec((tall, width), lambda i: (i, 0))
    return pl.pallas_call(
        encode_kernel,
        out_shape=jax.ShapeDtypeStruct(base.shape, BF16),
        grid=(2,),
        in_specs=[spec, spec],
        out_specs=spec,
        cost_estimate=pl.CostEstimate(
            flops=40 * base.size, bytes_accessed=8 * base.size, transcendentals=0
        ),
    )(base, weights)


def body(
    hidden_states, queries, token_ids, local_weights, outer_base, momentum, outer_rates, frag_index
):
    own = local_weights[0]
    place = lax.axis_index("fsdp")
    z, y, core = place // (Y_HI * CORES), (place // CORES) % Y_HI, place % CORES

    def near(dz, dy):
        return ((dz % Z, dy), ((z + dz) % Z) * Y_HI + (y + dy) % Y_HI)

    keys, vals = own[:, :HALF], own[:, HALF:]
    keys_across = send(keys, ACROSS)
    vals_up, vals_down = [send(vals, UP)], [send(vals, DOWN)]
    hidden_other = send(pick_columns(hidden_states, core[None]), SWAP)
    decoded = encode(outer_base, own)
    summed = lax.all_gather(
        decoded, "rep", axis_index_groups=[list(range(X)), list(range(X, 2 * X))]
    )
    cosine, sine, bias = tables(token_ids)

    pair = jnp.concatenate([keys, keys_across], axis=0)
    pair_up, pair_down = [send(pair, UP)], [send(pair, DOWN)]
    vals_, pair = tie(vals, pair)
    across = [send(vals_, ACROSS)]
    rotated = rotate_queries(queries, cosine, sine)
    vals_up.append(send(vals_up[0], UP))
    vals_down.append(send(vals_down[0], DOWN))
    both, across[0] = tie(jnp.concatenate([vals_up[0], vals_down[0]], axis=0), across[0])
    across.append(send(both, ACROSS))
    pair_up.append(send(pair_up[0], UP))
    pair_down.append(send(pair_down[0], DOWN))
    vals_up.append(send(vals_up[1], UP))
    vals_down.append(send(vals_down[1], DOWN))
    both, across[1] = tie(jnp.concatenate([vals_up[1], vals_down[1]], axis=0), across[1])
    across.append(send(both, ACROSS))
    pair_up.append(send(pair_up[1], UP))
    pair_down.append(send(pair_down[1], DOWN))
    vals_down.append(send(vals_down[2], DOWN))
    both, across[2] = tie(jnp.concatenate([vals_up[2], vals_down[2]], axis=0), across[2])
    across.append(send(both, ACROSS))
    pair_up.append(send(pair_up[2], UP))
    last, across[3] = tie(vals_down[3], across[3])
    across.append(send(last, ACROSS))

    def two(dz):
        return [near(dz, 0), near(dz, 1)]

    totals = multiply(
        hidden_states,
        hidden_other,
        [
            (two(0), 0, pair),
            (two(-1), 0, pair_up[0]),
            (two(1), 0, pair_down[0]),
            ([near(0, 0)], 1, vals),
            ([near(0, 1)], 1, across[0]),
            ([near(-1, 0)], 1, vals_up[0]),
            ([near(1, 0)], 1, vals_down[0]),
        ],
        core,
        None,
    )
    totals = multiply(
        hidden_states,
        hidden_other,
        [
            (two(-2), 0, pair_up[1]),
            (two(2), 0, pair_down[1]),
            ([near(-1, 1), near(1, 1)], 1, across[1]),
            ([near(-2, 0)], 1, vals_up[1]),
            ([near(2, 0)], 1, vals_down[1]),
        ],
        core,
        totals,
    )
    totals = multiply(
        hidden_states,
        hidden_other,
        [
            (two(-3), 0, pair_up[2]),
            (two(3), 0, pair_down[2]),
            ([near(-2, 1), near(2, 1)], 1, across[2]),
            ([near(-3, 0)], 1, vals_up[2]),
            ([near(3, 0)], 1, vals_down[2]),
        ],
        core,
        totals,
    )
    totals = multiply(
        hidden_states,
        hidden_other,
        [
            (two(-4), 0, pair_up[3]),
            ([near(-3, 1), near(3, 1)], 1, across[3]),
            ([near(4, 0)], 1, vals_down[3]),
            ([near(4, 1)], 1, across[4]),
        ],
        core,
        totals,
    )
    key_own, val_own, key_other, val_other = totals
    key_add, val_add = send(key_other, SWAP), send(val_other, SWAP)
    context = attend(rotated, key_own, key_add, val_own, val_add, cosine, sine, bias)

    groups = lax.axis_size("rep")
    part = jnp.sum(summed.astype(F32), axis=0).astype(BF16)
    rest = lax.ppermute(part, "rep", [(i, (i + X) % groups) for i in range(groups)])
    outer_grad = (part.astype(F32) + rest.astype(F32)) / groups
    table = jnp.arange(outer_rates.shape[0], dtype=jnp.int32)
    rate = jnp.sum(jnp.where(table == frag_index[0], outer_rates, 0.0))
    new_momentum = momentum_coef * momentum + outer_grad
    new_base = outer_base - rate * (outer_grad + momentum_coef * new_momentum)
    return (context, new_base, new_momentum)


def solution(mesh):
    placed = (
        P(("rep", "fsdp"), None),
        P(("rep", "fsdp"), None),
        P(("rep", "fsdp")),
        P("rep", "fsdp", None),
        P("fsdp", None),
        P("fsdp", None),
        P(),
        P(),
    )
    return jax.shard_map(
        body,
        mesh=mesh,
        in_specs=placed,
        out_specs=(P(("rep", "fsdp"), None), P("fsdp", None), P("fsdp", None)),
        check_vma=False,
    )
```

time: 244 us -> 153 us (0.63)
  waiting for transfers between devices: 144 us -> 34.8 us
  Pallas kernels: 0 us -> 44 us
  starting transfers between devices: 0.08 us -> 35.8 us
  blocking collectives: 24.9 us -> 0 us
  other arithmetic: 23.7 us -> 9.62 us
  matrix products: 11.8 us -> 0 us
  local copies, waits for them, and re-layouts: 23.6 us -> 12.4 us
    all_gather x2 -> x1, waiting for transfers between devices: 144 us -> 0.02 us  [body(): lax.all_gather(decoded, 'rep', axis_index_groups=[list(range(X)), list(ra...]
    pallas_call x0 -> x8, Pallas kernels: none -> 44 us  [the longest x4 15.3 us: multiply(): pl.pallas_call(functools.partial(multiply_kernel, n_h, uses), out_shape=[...]
    ppermute x0 -> x24, starting transfers between devices: none -> 35.7 us  [the longest x23 35.2 us: send(): return lax.ppermute(block, 'fsdp', pairs)]
    ppermute x0 -> x24, waiting for transfers between devices: none -> 34.8 us  [the longest x23 34.8 us: send(): return lax.ppermute(block, 'fsdp', pairs)]
    all_gather x1 -> x0, blocking collectives: 24.9 us -> none  [body(): lax.all_gather(scales[None], 'rep', axis=0, tiled=True)]
    dot_general x3 -> x0, matrix products: 11.8 us -> none  [the longest x1 9.49 us: body(): jnp.dot(hidden_states, lax.all_gather(own_weights, 'fsdp', axis=0, tiled=...]
    another operation x9 -> x0, other arithmetic: 7.13 us -> none
    slice x5 -> x1, local copies, waits for them, and re-layouts: 5.48 us -> 0.04 us  [body(): keys, vals = (own[:, :HALF], own[:, HALF:])]
  transfers between devices with their start and end apart: 2 -> 25, of which waited for: 2 -> 7; matrix products, arithmetic and copies ran while one was open for 12% -> 4% of each run, Pallas kernels for 0% -> 23%
where the time goes in v1:
time: 153 us; the launch traced here: 152 us
  Pallas kernels  44 us (29%)
  starting transfers between devices  35.8 us (23%)
  waiting for transfers between devices  34.8 us (23%)
  between operations  15 us (10%)
  local copies, waits for them, and re-layouts  12.4 us (8%)
  other arithmetic  9.62 us (6%)
    ppermute x23, starting transfers between devices, send(): return lax.ppermute(block, 'fsdp', pairs)  35.2 us
    ppermute x23, waiting for transfers between devices, send(): return lax.ppermute(block, 'fsdp', pairs)  34.8 us
    pallas_call x4, Pallas kernels, multiply(): pl.pallas_call(functools.partial(multiply_kernel, n_h, uses), out_shape=[...  15.3 us
    unnamed x62, local copies, waits for them, and re-layouts  12 us
    pallas_call x1, Pallas kernels, pick_columns(): pl.pallas_call(pick_kernel, out_shape=jax.ShapeDtypeStruct((TOK, blocks *...  9.51 us
    pallas_call x1, Pallas kernels, encode(): pl.pallas_call(encode_kernel, out_shape=jax.ShapeDtypeStruct(base.shape,...  8.47 us
    pallas_call x1, Pallas kernels, attend(): pl.pallas_call(attend_kernel, out_shape=jax.ShapeDtypeStruct(rotated.shap...  6.24 us
    pallas_call x1, Pallas kernels, rotate_queries(): pl.pallas_call(rotate_kernel, out_shape=jax.ShapeDtypeStruct(queries.shap...  4.44 us
  transfers between devices with their start and end apart: 25, of which 7 were waited for; matrix products, arithmetic and copies ran while one was open for 4% of the time, Pallas kernels for 23%

profile of v1, /device:TPU:1, one launch (start us, length us, event | category | flops | bytes accessed | tf_op | source)
XLA Modules:
  0.0 151.6 jit_solution(9800615546939327894)
XLA Ops:
  7.2 8.5 %shard_map.110 = bf16[256,1024]{1,0:T(8,128)(2,1)} custom-call(f32[256,1024]{1,0:T(8,128)} %base_ref.1, bf16[256,1024]{1,0:T(8,128)(2,1)} %bitcast.22), custom_call_target="tpu_custom_call" | custom-call | flops 10485760 | bytes 2097152 | tf_op jit(solution)/shard_map/pallas_call | solution.py:280
  15.8 3.8 %collective-permute-start.1 = (bf16[256,512]{1,0:T(8,128)(2,1)S(1)}, bf16[256,512]{1,0:T(8,128)(2,1)S(1)}, u32[]{:S(2)}, u32[]{:S(2)}) collective-permute-start(bf16[256,512]{1,0:T(8,128)(2,1)S(1)} %get-tuple-element.58), channel_id=1, source_target_pairs={{0,2},{1,3},{2,0},{3,1},{4,6},{5,7},{6,4},{7,5},{8,10},{9,11},{10,... | collective-permute-start | bytes 786440 | tf_op jit(solution)/shard_map/ppermute | solution.py:50
  21.2 3.9 %collective-permute-start.6 = (bf16[256,512]{1,0:T(8,128)(2,1)S(1)}, bf16[256,512]{1,0:T(8,128)(2,1)S(1)}, u32[]{:S(2)}, u32[]{:S(2)}) collective-permute-start(bf16[256,512]{1,0:T(8,128)(2,1)S(1)} %get-tuple-element.29.refs_15_), channel_id=1, source_target_pairs={{0,28},{1,29},{2,30},{3,31},{4,0},{5,1},{6,2},{7,3},{8,4},{9,5},{1... | collective-permute-start | bytes 786440 | tf_op jit(solution)/shard_map/ppermute | solution.py:50
  25.2 9.5 %shard_map.104 = bf16[256,4096]{1,0:T(8,128)(2,1)} custom-call(s32[1]{0:T(128)} %bitcast.4.core_ref, bf16[256,8192]{1,0:T(8,128)(2,1)} %refs_3_.7), custom_call_target="tpu_custom_call" | custom-call | bytes 4194304 | tf_op jit(solution)/shard_map/pallas_call | solution.py:63
  36.3 9.2 %collective-permute-done.13.refs_16_ = bf16[256,512]{1,0:T(8,128)(2,1)S(1)} collective-permute-done((bf16[256,512]{1,0:T(8,128)(2,1)S(1)}, bf16[256,512]{1,0:T(8,128)(2,1)S(1)}, u32[]{:S(2)}, u32[]{:S(2)}) %collective-permute-start.13) | collective-permute-done | bytes 262176 | tf_op jit(solution)/shard_map/ppermute | solution.py:50
  48.1 8.1 %collective-permute-done.11.refs_15_ = bf16[256,512]{1,0:T(8,128)(2,1)S(1)} collective-permute-done((bf16[256,512]{1,0:T(8,128)(2,1)S(1)}, bf16[256,512]{1,0:T(8,128)(2,1)S(1)}, u32[]{:S(2)}, u32[]{:S(2)}) %collective-permute-start.11) | collective-permute-done | bytes 262176 | tf_op jit(solution)/shard_map/ppermute | solution.py:50
  57.7 2.6 %collective-permute-done.14.refs_14_ = bf16[512,512]{1,0:T(8,128)(2,1)S(1)} collective-permute-done((bf16[512,512]{1,0:T(8,128)(2,1)S(1)}, bf16[512,512]{1,0:T(8,128)(2,1)S(1)}, u32[]{:S(2)}, u32[]{:S(2)}) %collective-permute-start.14) | collective-permute-done | bytes 524320 | tf_op jit(solution)/shard_map/ppermute | solution.py:50
  62.4 6.2 %collective-permute-done.18.refs_14_ = bf16[512,512]{1,0:T(8,128)(2,1)S(1)} collective-permute-done((bf16[512,512]{1,0:T(8,128)(2,1)S(1)}, bf16[512,512]{1,0:T(8,128)(2,1)S(1)}, u32[]{:S(2)}, u32[]{:S(2)}) %collective-permute-start.18) | collective-permute-done | bytes 524320 | tf_op jit(solution)/shard_map/ppermute | solution.py:50
  68.7 5.6 %collective-permute-done.8.refs_16_ = bf16[256,512]{1,0:T(8,128)(2,1)} collective-permute-done((bf16[256,512]{1,0:T(8,128)(2,1)S(1)}, bf16[256,512]{1,0:T(8,128)(2,1)}, u32[]{:S(2)}, u32[]{:S(2)}) %collective-permute-start.8) | collective-permute-done | bytes 262176 | tf_op jit(solution)/shard_map/ppermute | solution.py:50
  79.4 2.8 %collective-permute-start.16 = (bf16[512,512]{1,0:T(8,128)(2,1)}, bf16[512,512]{1,0:T(8,128)(2,1)}, u32[]{:S(2)}, u32[]{:S(2)}) collective-permute-start(bf16[512,512]{1,0:T(8,128)(2,1)} %pad_maximum_fusion.1), channel_id=1, source_target_pairs={{0,2},{1,3},{2,0},{3,1},{4,6},{5,7},{6,4},{7,5},{8,10},{9,11},{10,... | collective-permute-start | bytes 1572872 | tf_op jit(solution)/shard_map/ppermute | solution.py:50
  82.3 2.7 %collective-permute-start.9 = (bf16[256,512]{1,0:T(8,128)(2,1)}, bf16[256,512]{1,0:T(8,128)(2,1)}, u32[]{:S(2)}, u32[]{:S(2)}) collective-permute-start(bf16[256,512]{1,0:T(8,128)(2,1)} %collective-permute-done.8.refs_16_), channel_id=1, source_target_pairs={{0,28},{1,29},{2,30},{3,31},{4,0},{5,1},{6,2},{7,3},{8,4},{9,5},{1... | collective-permute-start | bytes 786440 | tf_op jit(solution)/shard_map/ppermute | solution.py:50
  85.8 3.0 %collective-permute-start.20 = (bf16[512,512]{1,0:T(8,128)(2,1)}, bf16[512,512]{1,0:T(8,128)(2,1)}, u32[]{:S(2)}, u32[]{:S(2)}) collective-permute-start(bf16[512,512]{1,0:T(8,128)(2,1)} %collective-permute-done.19.refs_13_), channel_id=1, source_target_pairs={{0,28},{1,29},{2,30},{3,31},{4,0},{5,1},{6,2},{7,3},{8,4},{9,5},{1... | collective-permute-start | bytes 1572872 | tf_op jit(solution)/shard_map/ppermute | solution.py:50
  89.3 2.3 %collective-permute-done.9.refs_10_ = bf16[256,512]{1,0:T(8,128)(2,1)} collective-permute-done((bf16[256,512]{1,0:T(8,128)(2,1)}, bf16[256,512]{1,0:T(8,128)(2,1)}, u32[]{:S(2)}, u32[]{:S(2)}) %collective-permute-start.9) | collective-permute-done | bytes 262176 | tf_op jit(solution)/shard_map/ppermute | solution.py:50
  91.5 2.7 %collective-permute-start.17 = (bf16[256,512]{1,0:T(8,128)(2,1)}, bf16[256,512]{1,0:T(8,128)(2,1)S(1)}, u32[]{:S(2)}, u32[]{:S(2)}) collective-permute-start(bf16[256,512]{1,0:T(8,128)(2,1)} %collective-permute-done.9.refs_10_), channel_id=1, source_target_pairs={{0,2},{1,3},{2,0},{3,1},{4,6},{5,7},{6,4},{7,5},{8,10},{9,11},{10,... | collective-permute-start | bytes 786440 | tf_op jit(solution)/shard_map/ppermute | solution.py:50
  94.3 2.2 %copy-done = bf16[256,8192]{1,0:T(8,128)(2,1)S(1)} copy-done((bf16[256,8192]{1,0:T(8,128)(2,1)S(1)}, bf16[256,8192]{1,0:T(8,128)(2,1)}, u32[]{:S(2)}) %copy-start) | copy-done | bytes 4194328
  102.4 2.9 %shard_map.105 = (f32[256,512]{1,0:T(8,128)S(1)}, f32[256,512]{1,0:T(8,128)S(1)}, f32[256,512]{1,0:T(8,128)}, f32[256,512]{1,0:T(8,128)}) custom-call(s32[7]{0:T(128)S(1)} %stack.92.index_ref, bf16[256,8192]{1,0:T(8,128)(2,1)S(1)} %copy-done, bf16[256,8192]{1,0:T(8,128)(2,1)S(1)} %copy-done, bf16[256,8192]{1,0:T(8,128)(2,1)S(1)} %copy-done, ...), custom_call_target="tpu_custom_call" | custom-call | flops 1342177280 | bytes 5242880 | tf_op jit(solution)/shard_map/pallas_call | solution.py:127
  105.4 4.3 %shard_map.106 = (f32[256,512]{1,0:T(8,128)S(1)}, f32[256,512]{1,0:T(8,128)S(1)}, f32[256,512]{1,0:T(8,128)}, f32[256,512]{1,0:T(8,128)}) custom-call(s32[7]{0:T(128)S(1)} %stack.87.index_ref, bf16[256,8192]{1,0:T(8,128)(2,1)S(1)} %copy-done, ...), custom_call_target="tpu_custom_call", output_to_operand_aliasing={{0}: (18, {}), {1}: (19, {}), {2}: (20, {}), {3}: (21, {})} | custom-call | flops 1073741824 | bytes 4194304 | tf_op jit(solution)/shard_map/pallas_call | solution.py:127
  109.6 4.3 %shard_map.107 = (f32[256,512]{1,0:T(8,128)S(1)}, f32[256,512]{1,0:T(8,128)S(1)}, f32[256,512]{1,0:T(8,128)}, f32[256,512]{1,0:T(8,128)}) custom-call(s32[7]{0:T(128)S(1)} %stack.82.index_ref, bf16[256,8192]{1,0:T(8,128)(2,1)S(1)} %copy-done, ...), custom_call_target="tpu_custom_call", output_to_operand_aliasing={{0}: (18, {}), {1}: (19, {}), {2}: (20, {}), {3}: (21, {})} | custom-call | flops 1073741824 | bytes 4194304 | tf_op jit(solution)/shard_map/pallas_call | solution.py:127
  113.9 3.9 %shard_map.108 = (f32[256,512]{1,0:T(8,128)S(1)}, f32[256,512]{1,0:T(8,128)S(1)}, f32[256,512]{1,0:T(8,128)}, f32[256,512]{1,0:T(8,128)}) custom-call(s32[5]{0:T(128)S(1)} %stack.77.index_ref, bf16[256,8192]{1,0:T(8,128)(2,1)S(1)} %copy-done, ...), custom_call_target="tpu_custom_call", output_to_operand_aliasing={{0}: (13, {}), {1}: (14, {}), {2}: (15, {}), {3}: (16, {})} | custom-call | flops 805306368 | bytes 3145728 | tf_op jit(solution)/shard_map/pallas_call | solution.py:127
  117.8 5.8 %collective-permute-start.21 = (f32[256,512]{1,0:T(8,128)}, f32[256,512]{1,0:T(8,128)S(1)}, u32[]{:S(2)}, u32[]{:S(2)}) collective-permute-start(f32[256,512]{1,0:T(8,128)} %get-tuple-element.52), channel_id=1, source_target_pairs={{0,1},{1,0},{2,3},{3,2},{4,5},{5,4},{6,7},{7,6},{8,9},{9,8},{10,11... | collective-permute-start | bytes 1572872 | tf_op jit(solution)/shard_map/ppermute | solution.py:50
  124.8 2.0 %reduce_sum.22 = bf16[256,1024]{1,0:T(8,128)(2,1)S(1)} reduce(bf16[4,256,1024]{2,1,0:T(8,128)(2,1)} %bitcast.21, bf16[]{:T(256)} %constant.185.clone.1), dimensions={0}, to_apply=%region_2.3 | reduce | flops 786432 | bytes 2621442 | tf_op jit(solution)/shard_map/reduce_sum | solution.py:397
  128.2 4.4 %shard_map.103.query_ref = bf16[256,4096]{1,0:T(8,128)(2,1)} custom-call(bf16[256,4096]{1,0:T(8,128)(2,1)} %query_ref.1, f32[256,128]{1,0:T(8,128)} %get-tuple-element.62.cos_ref, f32[256,128]{1,0:T(8,128)} %get-tuple-element.63.sin_ref), custom_call_target="tpu_custom_call" | custom-call | flops 4194304 | bytes 4194304 | tf_op jit(solution)/shard_map/pallas_call | solution.py:168
  135.0 6.2 %shard_map.109 = bf16[256,4096]{1,0:T(8,128)(2,1)} custom-call(bf16[256,4096]{1,0:T(8,128)(2,1)S(1)} %copy-done.1, f32[256,512]{1,0:T(8,128)S(1)} %get-tuple-element.51.key_ref, f32[256,512]{1,0:T(8,128)S(1)} %collective-permute-done.21.key_add_ref, f32[256,512]{1,0:T(8,128)S(1)} %get-tuple-element.53.val_ref, ...), custom_call_target="tpu_custom_call" | custom-call | flops 1073741824 | bytes 4194304 | tf_op jit(solution)/shard_map/pallas_call | solution.py:212
  141.3 3.5 %multiply_subtract_fusion = (f32[256,1024]{1,0:T(8,128)}, f32[256,1024]{1,0:T(8,128)}) fusion(f32[256,1024]{1,0:T(8,128)S(1)} %copy-done.26, bf16[256,1024]{1,0:T(8,128)(2,1)} %collective-permute-done.23, bf16[256,1024]{1,0:T(8,128)(2,1)S(1)} %reduce_sum.22, f32[]{:T(128)} %fusion.4, f32[256,1024]{1,0:T(8,128)S(1)} %copy-done.28), kind=kLoop, calls=%fused_computation | loop fusion | flops 2621440 | bytes 5242884 | tf_op jit(solution)/shard_map/sub | solution.py:403
  (116 shorter events, 26.2 us)
Async XLA Ops:
  7.2 117.6 %all-gather.3.cloned.1.call-start = ((), (), s32[]{:S(2)}) async-start(), calls=%async_computation | async-start | bytes 2621440 | tf_op jit(solution)/shard_map/all_gather | solution.py:307
  15.8 20.1 %collective-permute-start.1 = (bf16[256,512]{1,0:T(8,128)(2,1)S(1)}, bf16[256,512]{1,0:T(8,128)(2,1)S(1)}, u32[]{:S(2)}, u32[]{:S(2)}) collective-permute-start(bf16[256,512]{1,0:T(8,128)(2,1)S(1)} %get-tuple-element.58), channel_id=1, source_target_pairs={{0,2},{1,3},{2,0},{3,1},{4,6},{5,7},{6,4},{7,5},{8,10},{9,11},{10,... | collective-permute-start | bytes 786440 | tf_op jit(solution)/shard_map/ppermute | solution.py:50
  19.6 16.6 %collective-permute-start.10 = (bf16[256,512]{1,0:T(8,128)(2,1)S(1)}, bf16[256,512]{1,0:T(8,128)(2,1)S(1)}, u32[]{:S(2)}, u32[]{:S(2)}) collective-permute-start(bf16[256,512]{1,0:T(8,128)(2,1)S(1)} %get-tuple-element.29.refs_15_), channel_id=1, source_target_pairs={{0,4},{1,5},{2,6},{3,7},{4,8},{5,9},{6,10},{7,11},{8,12},{9,13},{1... | collective-permute-start | bytes 786440 | tf_op jit(solution)/shard_map/ppermute | solution.py:50
  21.2 15.0 %collective-permute-start.6 = (bf16[256,512]{1,0:T(8,128)(2,1)S(1)}, bf16[256,512]{1,0:T(8,128)(2,1)S(1)}, u32[]{:S(2)}, u32[]{:S(2)}) collective-permute-start(bf16[256,512]{1,0:T(8,128)(2,1)S(1)} %get-tuple-element.29.refs_15_), channel_id=1, source_target_pairs={{0,28},{1,29},{2,30},{3,31},{4,0},{5,1},{6,2},{7,3},{8,4},{9,5},{1... | collective-permute-start | bytes 786440 | tf_op jit(solution)/shard_map/ppermute | solution.py:50
  34.7 59.6 %collective-permute-start = (bf16[256,4096]{1,0:T(8,128)(2,1)}, bf16[256,4096]{1,0:T(8,128)(2,1)S(1)}, u32[]{:S(2)}, u32[]{:S(2)}) collective-permute-start(bf16[256,4096]{1,0:T(8,128)(2,1)} %shard_map.104), channel_id=1, source_target_pairs={{0,1},{1,0},{2,3},{3,2},{4,5},{5,4},{6,7},{7,6},{8,9},{9,8},{10,11... | collective-permute-start | bytes 6291464 | tf_op jit(solution)/shard_map/ppermute | solution.py:50
  36.0 9.5 %collective-permute-start.13 = (bf16[256,512]{1,0:T(8,128)(2,1)S(1)}, bf16[256,512]{1,0:T(8,128)(2,1)S(1)}, u32[]{:S(2)}, u32[]{:S(2)}) collective-permute-start(bf16[256,512]{1,0:T(8,128)(2,1)S(1)} %get-tuple-element.29.refs_15_), channel_id=1, source_target_pairs={{0,2},{1,3},{2,0},{3,1},{4,6},{5,7},{6,4},{7,5},{8,10},{9,11},{10,... | collective-permute-start | bytes 786440 | tf_op jit(solution)/shard_map/ppermute | solution.py:50
  36.1 20.7 %collective-permute-start.2 = (bf16[512,512]{1,0:T(8,128)(2,1)S(1)}, bf16[512,512]{1,0:T(8,128)(2,1)S(1)}, u32[]{:S(2)}, u32[]{:S(2)}) collective-permute-start(bf16[512,512]{1,0:T(8,128)(2,1)S(1)} %pad_maximum_fusion.refs_12_), channel_id=1, source_target_pairs={{0,4},{1,5},{2,6},{3,7},{4,8},{5,9},{6,10},{7,11},{8,12},{9,13},{1... | collective-permute-start | bytes 1572872 | tf_op jit(solution)/shard_map/ppermute | solution.py:50
  36.2 20.0 %collective-permute-start.11 = (bf16[256,512]{1,0:T(8,128)(2,1)S(1)}, bf16[256,512]{1,0:T(8,128)(2,1)S(1)}, u32[]{:S(2)}, u32[]{:S(2)}) collective-permute-start(bf16[256,512]{1,0:T(8,128)(2,1)S(1)} %collective-permute-done.10.refs_17_), channel_id=1, source_target_pairs={{0,4},{1,5},{2,6},{3,7},{4,8},{5,9},{6,10},{7,11},{8,12},{9,13},{1... | collective-permute-start | bytes 786440 | tf_op jit(solution)/shard_map/ppermute | solution.py:50
  46.2 14.2 %collective-permute-start.14 = (bf16[512,512]{1,0:T(8,128)(2,1)S(1)}, bf16[512,512]{1,0:T(8,128)(2,1)S(1)}, u32[]{:S(2)}, u32[]{:S(2)}) collective-permute-start(bf16[512,512]{1,0:T(8,128)(2,1)S(1)} %pad_maximum_fusion.3), channel_id=1, source_target_pairs={{0,2},{1,3},{2,0},{3,1},{4,6},{5,7},{6,4},{7,5},{8,10},{9,11},{10,... | collective-permute-start | bytes 1572872 | tf_op jit(solution)/shard_map/ppermute | solution.py:50
  46.4 11.3 %collective-permute-start.7 = (bf16[256,512]{1,0:T(8,128)(2,1)S(1)}, bf16[256,512]{1,0:T(8,128)(2,1)S(1)}, u32[]{:S(2)}, u32[]{:S(2)}) collective-permute-start(bf16[256,512]{1,0:T(8,128)(2,1)S(1)} %collective-permute-done.6.refs_18_), channel_id=1, source_target_pairs={{0,28},{1,29},{2,30},{3,31},{4,0},{5,1},{6,2},{7,3},{8,4},{9,5},{1... | collective-permute-start | bytes 786440 | tf_op jit(solution)/shard_map/ppermute | solution.py:50
  56.2 12.4 %collective-permute-start.18 = (bf16[512,512]{1,0:T(8,128)(2,1)S(1)}, bf16[512,512]{1,0:T(8,128)(2,1)S(1)}, u32[]{:S(2)}, u32[]{:S(2)}) collective-permute-start(bf16[512,512]{1,0:T(8,128)(2,1)S(1)} %pad_maximum_fusion.refs_12_), channel_id=1, source_target_pairs={{0,28},{1,29},{2,30},{3,31},{4,0},{5,1},{6,2},{7,3},{8,4},{9,5},{1... | collective-permute-start | bytes 1572872 | tf_op jit(solution)/shard_map/ppermute | solution.py:50
  56.8 19.3 %collective-permute-start.3 = (bf16[512,512]{1,0:T(8,128)(2,1)S(1)}, bf16[512,512]{1,0:T(8,128)(2,1)}, u32[]{:S(2)}, u32[]{:S(2)}) collective-permute-start(bf16[512,512]{1,0:T(8,128)(2,1)S(1)} %collective-permute-done.2.refs_13_), channel_id=1, source_target_pairs={{0,4},{1,5},{2,6},{3,7},{4,8},{5,9},{6,10},{7,11},{8,12},{9,13},{1... | collective-permute-start | bytes 1572872 | tf_op jit(solution)/shard_map/ppermute | solution.py:50
  60.4 18.2 %collective-permute-start.15 = (bf16[512,512]{1,0:T(8,128)(2,1)S(1)}, bf16[512,512]{1,0:T(8,128)(2,1)S(1)}, u32[]{:S(2)}, u32[]{:S(2)}) collective-permute-start(bf16[512,512]{1,0:T(8,128)(2,1)S(1)} %pad_maximum_fusion.2), channel_id=1, source_target_pairs={{0,2},{1,3},{2,0},{3,1},{4,6},{5,7},{6,4},{7,5},{8,10},{9,11},{10,... | collective-permute-start | bytes 1572872 | tf_op jit(solution)/shard_map/ppermute | solution.py:50
  60.7 13.6 %collective-permute-start.8 = (bf16[256,512]{1,0:T(8,128)(2,1)S(1)}, bf16[256,512]{1,0:T(8,128)(2,1)}, u32[]{:S(2)}, u32[]{:S(2)}) collective-permute-start(bf16[256,512]{1,0:T(8,128)(2,1)S(1)} %collective-permute-done.7.refs_16_), channel_id=1, source_target_pairs={{0,28},{1,29},{2,30},{3,31},{4,0},{5,1},{6,2},{7,3},{8,4},{9,5},{1... | collective-permute-start | bytes 786440 | tf_op jit(solution)/shard_map/ppermute | solution.py:50
  74.3 11.5 %collective-permute-start.19 = (bf16[512,512]{1,0:T(8,128)(2,1)S(1)}, bf16[512,512]{1,0:T(8,128)(2,1)}, u32[]{:S(2)}, u32[]{:S(2)}) collective-permute-start(bf16[512,512]{1,0:T(8,128)(2,1)S(1)} %collective-permute-done.18.refs_14_), channel_id=1, source_target_pairs={{0,28},{1,29},{2,30},{3,31},{4,0},{5,1},{6,2},{7,3},{8,4},{9,5},{1... | collective-permute-start | bytes 1572872 | tf_op jit(solution)/shard_map/ppermute | solution.py:50
  76.1 13.1 %collective-permute-start.4 = (bf16[512,512]{1,0:T(8,128)(2,1)}, bf16[512,512]{1,0:T(8,128)(2,1)}, u32[]{:S(2)}, u32[]{:S(2)}) collective-permute-start(bf16[512,512]{1,0:T(8,128)(2,1)} %collective-permute-done.3.refs_12_), channel_id=1, source_target_pairs={{0,4},{1,5},{2,6},{3,7},{4,8},{5,9},{6,10},{7,11},{8,12},{9,13},{1... | collective-permute-start | bytes 1572872 | tf_op jit(solution)/shard_map/ppermute | solution.py:50
  79.4 12.2 %collective-permute-start.16 = (bf16[512,512]{1,0:T(8,128)(2,1)}, bf16[512,512]{1,0:T(8,128)(2,1)}, u32[]{:S(2)}, u32[]{:S(2)}) collective-permute-start(bf16[512,512]{1,0:T(8,128)(2,1)} %pad_maximum_fusion.1), channel_id=1, source_target_pairs={{0,2},{1,3},{2,0},{3,1},{4,6},{5,7},{6,4},{7,5},{8,10},{9,11},{10,... | collective-permute-start | bytes 1572872 | tf_op jit(solution)/shard_map/ppermute | solution.py:50
  82.3 9.3 %collective-permute-start.9 = (bf16[256,512]{1,0:T(8,128)(2,1)}, bf16[256,512]{1,0:T(8,128)(2,1)}, u32[]{:S(2)}, u32[]{:S(2)}) collective-permute-start(bf16[256,512]{1,0:T(8,128)(2,1)} %collective-permute-done.8.refs_16_), channel_id=1, source_target_pairs={{0,28},{1,29},{2,30},{3,31},{4,0},{5,1},{6,2},{7,3},{8,4},{9,5},{1... | collective-permute-start | bytes 786440 | tf_op jit(solution)/shard_map/ppermute | solution.py:50
  85.8 23.8 %collective-permute-start.20 = (bf16[512,512]{1,0:T(8,128)(2,1)}, bf16[512,512]{1,0:T(8,128)(2,1)}, u32[]{:S(2)}, u32[]{:S(2)}) collective-permute-start(bf16[512,512]{1,0:T(8,128)(2,1)} %collective-permute-done.19.refs_13_), channel_id=1, source_target_pairs={{0,28},{1,29},{2,30},{3,31},{4,0},{5,1},{6,2},{7,3},{8,4},{9,5},{1... | collective-permute-start | bytes 1572872 | tf_op jit(solution)/shard_map/ppermute | solution.py:50
  89.2 24.7 %collective-permute-start.5 = (bf16[512,512]{1,0:T(8,128)(2,1)}, bf16[512,512]{1,0:T(8,128)(2,1)S(1)}, u32[]{:S(2)}, u32[]{:S(2)}) collective-permute-start(bf16[512,512]{1,0:T(8,128)(2,1)} %collective-permute-done.4.refs_12_), channel_id=1, source_target_pairs={{0,4},{1,5},{2,6},{3,7},{4,8},{5,9},{6,10},{7,11},{8,12},{9,13},{1... | collective-permute-start | bytes 1572872 | tf_op jit(solution)/shard_map/ppermute | solution.py:50
  91.5 22.4 %collective-permute-start.17 = (bf16[256,512]{1,0:T(8,128)(2,1)}, bf16[256,512]{1,0:T(8,128)(2,1)S(1)}, u32[]{:S(2)}, u32[]{:S(2)}) collective-permute-start(bf16[256,512]{1,0:T(8,128)(2,1)} %collective-permute-done.9.refs_10_), channel_id=1, source_target_pairs={{0,2},{1,3},{2,0},{3,1},{4,6},{5,7},{6,4},{7,5},{8,10},{9,11},{10,... | collective-permute-start | bytes 786440 | tf_op jit(solution)/shard_map/ppermute | solution.py:50
  117.8 15.5 %collective-permute-start.21 = (f32[256,512]{1,0:T(8,128)}, f32[256,512]{1,0:T(8,128)S(1)}, u32[]{:S(2)}, u32[]{:S(2)}) collective-permute-start(f32[256,512]{1,0:T(8,128)} %get-tuple-element.52), channel_id=1, source_target_pairs={{0,1},{1,0},{2,3},{3,2},{4,5},{5,4},{6,7},{7,6},{8,9},{9,8},{10,11... | collective-permute-start | bytes 1572872 | tf_op jit(solution)/shard_map/ppermute | solution.py:50
  123.6 9.8 %collective-permute-start.22 = (f32[256,512]{1,0:T(8,128)}, f32[256,512]{1,0:T(8,128)S(1)}, u32[]{:S(2)}, u32[]{:S(2)}) collective-permute-start(f32[256,512]{1,0:T(8,128)} %get-tuple-element.54), channel_id=1, source_target_pairs={{0,1},{1,0},{2,3},{3,2},{4,5},{5,4},{6,7},{7,6},{8,9},{9,8},{10,11... | collective-permute-start | bytes 1572872 | tf_op jit(solution)/shard_map/ppermute | solution.py:50
  126.8 14.4 %collective-permute-start.23 = (bf16[256,1024]{1,0:T(8,128)(2,1)S(1)}, bf16[256,1024]{1,0:T(8,128)(2,1)}, u32[]{:S(2)}, u32[]{:S(2)}) collective-permute-start(bf16[256,1024]{1,0:T(8,128)(2,1)S(1)} %reduce_sum.22), channel_id=1, source_target_pairs={{0,128},{32,160},{64,192},{96,224},{128,0},{160,32},{192,64},{224,... | collective-permute-start | bytes 1572872 | tf_op jit(solution)/shard_map/ppermute | solution.py:398
  (32 other events, 383.7 us)
Sparse Core Ops, SparseCore 0:
  15.8 37.1 all-gather.2

commit v2 on v1

v2 whole, which is shorter than its diff:
```python
import functools
import math

import jax
import jax.numpy as jnp
from jax import lax
from jax.experimental import pallas as pl
from jax.experimental.pallas import tpu as pltpu
from jax.sharding import PartitionSpec as P

HEAD = 128
BLOCK = 32
BOS = 128000
TOK = 256
ROWS = 256
KV_HEADS = 4
HALF = KV_HEADS * HEAD
GROUP_HEADS = 8
Z, Y_HI, CORES = 8, 2, 2
X = 4

rope_base = 500000.0
momentum_coef = 0.9
F32 = jnp.float32
BF16 = jnp.bfloat16

NO_COST = pl.CostEstimate(flops=0, bytes_accessed=0, transcendentals=0)


def fsdp_pairs(move):
    pairs = []
    for z in range(Z):
        for y in range(Y_HI):
            for c in range(CORES):
                z2, y2, c2 = move(z, y, c)
                pairs.append(
                    (
                        (z * Y_HI + y) * CORES + c,
                        ((z2 % Z) * Y_HI + y2 % Y_HI) * CORES + c2 % CORES,
                    )
                )
    return pairs


UP = fsdp_pairs(lambda z, y, c: (z + 1, y, c))
DOWN = fsdp_pairs(lambda z, y, c: (z - 1, y, c))
ACROSS = fsdp_pairs(lambda z, y, c: (z, y + 1, c))
SWAP = fsdp_pairs(lambda z, y, c: (z, y, c + 1))


def send(block, pairs):
    return lax.ppermute(block, "fsdp", pairs)


def tie(*arrays):
    return lax.optimization_barrier(arrays)


def collect_kernel(moves, n_in, *refs):
    sources, (*outs, sems) = refs[:n_in], refs[n_in:]
    copies = []
    for i, (source, col, out, at) in enumerate(moves):
        copies.append(
            pltpu.make_async_copy(
                sources[source].at[:, pl.ds(col, HALF)],
                outs[out].at[pl.ds(at, ROWS), :],
                sems.at[i],
            )
        )
        copies[-1].start()
    for copy in copies:
        copy.wait()


def collect(sources, outs):
    moves = []
    for out, pieces in enumerate(outs):
        for i, (source, col) in enumerate(pieces):
            moves.append((source, col, out, i * ROWS))
    return pl.pallas_call(
        functools.partial(collect_kernel, moves, len(sources)),
        out_shape=[jax.ShapeDtypeStruct((len(p) * ROWS, HALF), BF16) for p in outs],
        in_specs=[pl.BlockSpec(memory_space=pltpu.HBM)] * len(sources),
        out_specs=[pl.BlockSpec(memory_space=pltpu.VMEM)] * len(outs),
        scratch_shapes=[pltpu.SemaphoreType.DMA((len(moves),))],
        cost_estimate=NO_COST,
        compiler_params=pltpu.CompilerParams(vmem_limit_bytes=2 * 2**20),
    )(*sources)


def block_place(place_ref, dz, dy):
    z, y, core = place_ref[0], place_ref[1], place_ref[2]
    return (lax.rem(z + dz + Z, Z) * Y_HI + lax.rem(y + dy, Y_HI)) * CORES + core


def multiply_kernel(blocks, moves, spans, n_w, add, ahead, place_ref, *refs):
    hidden = refs[:2]
    weights = refs[2 : 2 + n_w]
    before = refs[2 + n_w : 2 + n_w + add]
    out_ref = refs[2 + n_w + add]
    if ahead:
        ahead_ref = refs[3 + n_w + add]
        refs = refs[4 + n_w + add :]
    else:
        refs = refs[3 + n_w + add :]
    states, stacks, (held, out_sems, sems) = refs[0], refs[1:3], refs[3:]
    count = iter(range(sems.shape[0]))

    def begin(source, target):
        copy = pltpu.make_async_copy(source, target, sems.at[next(count)])
        copy.start()
        return copy

    def fetch(block, target, slot):
        start = pl.multiple_of(block_place(place_ref, *block) * ROWS, ROWS)
        return [
            begin(
                hidden[side].at[:, pl.ds(start, ROWS)],
                target.at[pl.ds(side * TOK, TOK), pl.ds(slot * ROWS, ROWS)],
            )
            for side in range(2)
        ]

    ready = []
    for slot, block in enumerate(blocks):
        ready += fetch(block, states, slot)
    parts = []
    for part in range(2):
        copies = []
        for piece, row, col, slot in moves[part]:
            copies.append(
                begin(
                    weights[piece].at[pl.ds(row, ROWS), pl.ds(col, HALF)],
                    stacks[part].at[pl.ds(slot, ROWS), :],
                )
            )
        if add:
            copies.append(begin(before[0].at[part], held.at[part]))
        parts.append(copies)
    later = []
    for slot, block in enumerate(ahead):
        later += fetch(block, ahead_ref, slot)
    for copy in ready:
        copy.wait()
    leaving = []
    for part in range(2):
        for copy in parts[part]:
            copy.wait()
        first, last = spans[part]
        for half in range(2):
            cols = slice(half * ROWS, (half + 1) * ROWS)
            total = jnp.dot(
                states[:, first * ROWS : last * ROWS],
                stacks[part][:, cols],
                preferred_element_type=F32,
            )
            if add:
                total = total + held[part, :, cols]
            if ahead:
                out_ref[part, :, cols] = total
            else:
                held[part, :, cols] = total
        if not ahead:
            copy = pltpu.make_async_copy(held.at[part], out_ref.at[part], out_sems.at[part])
            copy.start()
            leaving.append(copy)
    for copy in later + leaving:
        copy.wait()


def multiply(hidden, hidden_other, blocks, pieces, place, total=None, ahead=()):
    weights, moves, spans = [], [], []
    for which, part in enumerate(pieces):
        slots = [slot for _, places in part for slot in places]
        first, last = min(slots), max(slots) + 1
        assert sorted(slots) == list(range(first, last))
        spans.append((first, last))
        moves.append([])
        for rows, places in part:
            col = which * HALF if rows.shape[1] > HALF else 0
            for i, slot in enumerate(places):
                moves[-1].append((len(weights), i * ROWS, col, (slot - first) * ROWS))
            weights.append(rows)
    n_h, n_w, n_a = len(blocks), len(weights), len(ahead)
    add = 0 if total is None else 1
    far = pl.BlockSpec(memory_space=pltpu.HBM)
    near = pl.BlockSpec(memory_space=pltpu.VMEM)
    n_sems = 2 * (n_h + n_a) + sum(len(m) for m in moves) + 2 * add
    scratch = [pltpu.VMEM((2 * TOK, n_h * ROWS), BF16)]
    scratch += [pltpu.VMEM(((last - first) * ROWS, HALF), BF16) for first, last in spans]
    scratch += [
        pltpu.VMEM((2, 2 * TOK, HALF), F32),
        pltpu.SemaphoreType.DMA((2,)),
        pltpu.SemaphoreType.DMA((n_sems,)),
    ]
    out_shape = [jax.ShapeDtypeStruct((2, 2 * TOK, HALF), F32)]
    if ahead:
        out_shape.append(jax.ShapeDtypeStruct((2 * TOK, n_a * ROWS), BF16))
    return pl.pallas_call(
        functools.partial(multiply_kernel, blocks, moves, spans, n_w, add, ahead),
        out_shape=out_shape,
        in_specs=[pl.BlockSpec(memory_space=pltpu.SMEM)] + [far] * (2 + n_w + add),
        out_specs=[near] * 2 if ahead else [far],
        scratch_shapes=scratch,
        cost_estimate=NO_COST,
        compiler_params=pltpu.CompilerParams(vmem_limit_bytes=(48 if ahead else 60) * 2**20),
    )(place, hidden, hidden_other, *weights, *([total] * add))


def finish_kernel(
    states_ref, total_ref, near_ref, far_ref, val_in_ref,
    key_ref, val_ref, key_swap_ref, val_swap_ref
):
    uses = ((near_ref, 0, 0), (far_ref, 0, 1), (val_in_ref, 1, 0))
    outs = ((key_ref, key_swap_ref), (val_ref, val_swap_ref))
    for part in range(2):
        for half in range(2):
            cols = slice(half * ROWS, (half + 1) * ROWS)
            total = total_ref[part, :, cols]
            for ref, where, slot in uses:
                if where == part:
                    total = total + jnp.dot(
                        states_ref[:, slot * ROWS : (slot + 1) * ROWS],
                        ref[:, cols],
                        preferred_element_type=F32,
                    )
            mine_ref, swap_ref = outs[part]
            mine_ref[:, cols] = total[:TOK]
            swap_ref[:, cols] = total[TOK:].astype(swap_ref.dtype)


def finish(states, total, keys_near, keys_far, vals):
    near = pl.BlockSpec(memory_space=pltpu.VMEM)
    return pl.pallas_call(
        finish_kernel,
        out_shape=[
            jax.ShapeDtypeStruct((TOK, HALF), F32),
            jax.ShapeDtypeStruct((TOK, HALF), F32),
            jax.ShapeDtypeStruct((TOK, HALF), F32),
            jax.ShapeDtypeStruct((TOK, HALF), BF16),
        ],
        in_specs=[near] * 5,
        out_specs=[near] * 4,
        cost_estimate=NO_COST,
        compiler_params=pltpu.CompilerParams(vmem_limit_bytes=6 * 2**20),
    )(states, total, keys_near, keys_far, vals)


def rope(head, cosine, sine):
    return head * cosine + pltpu.roll(head, HEAD // 2, 1) * sine


def rotate_kernel(query_ref, cos_ref, sin_ref, out_ref):
    for h in range(GROUP_HEADS):
        cols = slice(h * HEAD, (h + 1) * HEAD)
        out_ref[:, cols] = rope(
            query_ref[:, cols].astype(F32), cos_ref[...], sin_ref[...]
        ).astype(BF16)


def rotate_queries(queries, cosine, sine):
    width = GROUP_HEADS * HEAD
    spec = pl.BlockSpec((TOK, width), lambda h: (0, h))
    table = pl.BlockSpec((TOK, HEAD), lambda h: (0, 0))
    return pl.pallas_call(
        rotate_kernel,
        out_shape=jax.ShapeDtypeStruct(queries.shape, BF16),
        grid=(KV_HEADS,),
        in_specs=[spec, table, table],
        out_specs=spec,
        cost_estimate=NO_COST,
        compiler_params=pltpu.CompilerParams(vmem_limit_bytes=6 * 2**20),
    )(queries, cosine, sine)


def attend_kernel(
    query_ref, key_ref, key_add_ref, val_ref, val_add_ref, cos_ref, sin_ref, bias_ref, out_ref
):
    keys = rope(key_ref[...] + key_add_ref[...], cos_ref[...], sin_ref[...]).astype(BF16)
    vals = (val_ref[...] + val_add_ref[...].astype(F32)).astype(BF16)
    vals = jnp.concatenate([vals, jnp.ones((TOK, HEAD), BF16)], axis=1)
    factor = math.log2(math.e) / math.sqrt(HEAD)
    part = TOK // 2
    for r in range(2):
        rows = slice(r * part, (r + 1) * part)
        seen = (r + 1) * part
        heads = [query_ref[rows, h * HEAD : (h + 1) * HEAD] for h in range(GROUP_HEADS)]
        scores = lax.dot_general(
            jnp.concatenate(heads, axis=0),
            keys[:seen],
            (((1,), (1,)), ((), ())),
            preferred_element_type=F32,
        )
        scores = scores.reshape(GROUP_HEADS, part, seen) + bias_ref[rows, :seen][None]
        peak = jnp.max(scores, axis=2, keepdims=True)
        weights = jnp.exp2((scores - peak) * factor).astype(BF16)
        both = jnp.dot(
            weights.reshape(GROUP_HEADS * part, seen),
            vals[:seen],
            preferred_element_type=F32,
        )
        context = (both[:, :HEAD] / both[:, HEAD:]).astype(BF16)
        for h in range(GROUP_HEADS):
            out_ref[rows, h * HEAD : (h + 1) * HEAD] = context[h * part : (h + 1) * part]


def attend(rotated, keys, keys_add, vals, vals_add, cosine, sine, bias):
    width = GROUP_HEADS * HEAD
    wide = pl.BlockSpec((TOK, width), lambda h: (0, h))
    one = pl.BlockSpec((TOK, HEAD), lambda h: (0, h))
    table = pl.BlockSpec((TOK, HEAD), lambda h: (0, 0))
    square = pl.BlockSpec((TOK, TOK), lambda h: (0, 0))
    return pl.pallas_call(
        attend_kernel,
        out_shape=jax.ShapeDtypeStruct(rotated.shape, BF16),
        grid=(KV_HEADS,),
        in_specs=[wide, one, one, one, one, table, table, square],
        out_specs=wide,
        cost_estimate=NO_COST,
        compiler_params=pltpu.CompilerParams(vmem_limit_bytes=12 * 2**20),
    )(rotated, keys, keys_add, vals, vals_add, cosine, sine, bias)


def tables(token_row):
    token = jnp.arange(TOK, dtype=jnp.int32)
    started = (token_row == BOS)[None, :] & (token[None, :] <= token[:, None])
    latest = jnp.max(jnp.where(started, token[None, :], 0), axis=1)
    positions = (token - latest).astype(F32)
    steps = jnp.arange(HEAD // 2, dtype=F32)
    inverse = rope_base ** (-2.0 * steps / HEAD)
    angles = positions[:, None] * inverse[None, :]
    cosine, sine = jnp.cos(angles), jnp.sin(angles)
    allowed = (token[None, :] <= token[:, None]) & (token[None, :] >= latest[:, None])
    bias = jnp.where(allowed, 0.0, -1e30).astype(F32)
    return (
        jnp.concatenate([cosine, cosine], axis=1),
        jnp.concatenate([-sine, sine], axis=1),
        bias,
    )


def top_bit(number):
    return 31 - lax.clz(jnp.maximum(number, 1))


def power(exponent):
    return lax.shift_left(jnp.full(exponent.shape, 1, jnp.int32), exponent).astype(F32)


def encode_kernel(base_ref, weight_ref, out_ref):
    lanes = lax.broadcasted_iota(jnp.int32, (base_ref.shape[0], HEAD), 1)
    for j in range(base_ref.shape[1] // HEAD):
        cols = slice(j * HEAD, (j + 1) * HEAD)
        delta = base_ref[:, cols] - weight_ref[:, cols].astype(F32)
        size = jnp.abs(delta)
        peak = size
        for reach in (1, 2, 4, 8, 16):
            peak = jnp.maximum(peak, pltpu.roll(peak, reach, 1))
        peak = jnp.take_along_axis(peak, lanes | (BLOCK - 1), axis=1)
        block = top_bit((peak * 2.0**30).astype(jnp.int32))
        value = (size * (power(30 - block) * 2.0**29)).astype(jnp.int32)
        step = jnp.maximum(top_bit(value), 15) - 3
        half = lax.shift_left(jnp.full(step.shape, 1, jnp.int32), step - 1)
        counted = lax.shift_right_logical(value + half, step)
        value = jnp.minimum(lax.shift_left(counted, step), 448 * 2**21)
        code = value.astype(F32) * (power(block) * 2.0**-59)
        out_ref[:, cols] = jnp.where(delta < 0, -code, code).astype(BF16)


def encode(base, weights):
    rows, width = base.shape
    tall = rows // 2
    spec = pl.BlockSpec((tall, width), lambda i: (i, 0))
    return pl.pallas_call(
        encode_kernel,
        out_shape=jax.ShapeDtypeStruct(base.shape, BF16),
        grid=(2,),
        in_specs=[spec, spec],
        out_specs=spec,
        cost_estimate=NO_COST,
        compiler_params=pltpu.CompilerParams(vmem_limit_bytes=6 * 2**20),
    )(base, weights)


def body(
    hidden_states, queries, token_ids, local_weights, outer_base, momentum, outer_rates, frag_index
):
    own = local_weights[0]
    place = lax.axis_index("fsdp")
    z, y, core = place // (Y_HI * CORES), (place // CORES) % Y_HI, place % CORES

    place = jnp.stack([z, y, core]).astype(jnp.int32)

    groups = lax.axis_size("rep")

    def along_x(pick):
        return [(i, i // X * X + pick(i % X)) for i in range(groups)]

    def add(mine, theirs):
        return (mine.astype(F32) + theirs.astype(F32)).astype(BF16)

    hidden_other = send(hidden_states, SWAP)
    up, down = [send(own, UP)], [send(own, DOWN)]
    keys_across = send(own[:, :HALF], ACROSS)
    across = [send(own[:, HALF:], ACROSS)]

    def halves(*blocks):
        return collect(blocks, [[(i, HALF) for i in range(len(blocks))]])[0]

    hidden_other, own_ = tie(hidden_other, own)
    decoded = encode(outer_base, own_)
    up[0], down[0], keys_across, decoded, queries, token_ids = tie(
        up[0], down[0], keys_across, decoded, queries, token_ids
    )
    up.append(send(up[0], UP))
    down.append(send(down[0], DOWN))
    far_up = [send(keys_across, UP)]
    rest = lax.ppermute(decoded, "rep", along_x(lambda x: x ^ 1))
    across.append(send(halves(up[0], down[0]), ACROSS))

    cosine, sine, bias = tables(token_ids)
    table = jnp.arange(outer_rates.shape[0], dtype=jnp.int32)
    rate = jnp.sum(jnp.where(table == frag_index[0], outer_rates, 0.0))
    rotated = rotate_queries(queries, cosine, sine)

    (total,) = multiply(
        hidden_states,
        hidden_other,
        [(0, 0), (0, 1), (-1, 0), (1, 0)],
        [
            [(own, (0,)), (keys_across, (1,)), (up[0], (2,)), (down[0], (3,))],
            [(own, (0,)), (across[0], (1,)), (up[0], (2,)), (down[0], (3,))],
        ],
        place,
    )
    up[1], down[1], rotated, total, rate = tie(up[1], down[1], rotated, total, rate)
    up.append(send(up[1], UP))
    down.append(send(down[1], DOWN))
    up[1], down[1], far_up[0], across[1], rest, keys_across = tie(
        up[1], down[1], far_up[0], across[1], rest, keys_across
    )
    far_up.append(send(far_up[0], UP))
    far_down = [send(keys_across, DOWN)]
    across.append(send(halves(up[1], down[1]), ACROSS))
    part = add(decoded, rest)
    (total,) = multiply(
        hidden_states,
        hidden_other,
        [(-1, 1), (-2, 0), (2, 0), (1, 1)],
        [
            [(far_up[0], (0,)), (up[1], (1,)), (down[1], (2,))],
            [(across[1], (0, 3)), (up[1], (1,)), (down[1], (2,))],
        ],
        place,
        total,
    )
    up[2], down[2], total, part = tie(up[2], down[2], total, part)
    val_last, key_last, vals = collect(
        (up[2], down[2]), [[(0, HALF)], [(1, 0)], [(0, HALF), (1, HALF)]]
    )
    val_last = send(val_last, UP)
    key_last = send(key_last, DOWN)
    up[2], down[2], far_up[1], far_down[0], across[2], vals = tie(
        up[2], down[2], far_up[1], far_down[0], across[2], vals
    )
    far_up.append(send(far_up[1], UP))
    far_down.append(send(far_down[0], DOWN))
    across.append(send(vals, ACROSS))

    (total,) = multiply(
        hidden_states,
        hidden_other,
        [(1, 1), (-2, 1), (-3, 0), (3, 0), (2, 1)],
        [
            [(far_down[0], (0,)), (far_up[1], (1,)), (up[2], (2,)), (down[2], (3,))],
            [(across[2], (1, 4)), (up[2], (2,)), (down[2], (3,))],
        ],
        place,
        total,
    )
    val_last, key_last, total = tie(val_last, key_last, total)
    across.append(send(val_last, ACROSS))
    val_last, key_last, far_up[2], far_down[1], across[3], part = tie(
        val_last, key_last, far_up[2], far_down[1], across[3], part
    )
    far_up.append(send(far_up[2], UP))
    far_down.append(send(far_down[1], DOWN))
    rest = lax.ppermute(part, "rep", along_x(lambda x: X - 1 - x))
    total, states = multiply(
        hidden_states,
        hidden_other,
        [(2, 1), (-3, 1), (4, 0), (3, 1)],
        [
            [(far_down[1], (0,)), (far_up[2], (1,)), (key_last, (2,))],
            [(across[3], (1, 3)), (val_last, (2,))],
        ],
        place,
        total,
        ahead=((4, 1), (3, 1)),
    )
    key_own, val_own, key_swap, val_swap = finish(
        states, total, far_up[3], far_down[2], across[4]
    )
    rest, key_own = tie(rest, key_own)
    part = add(part, rest)
    rest = lax.ppermute(part, "rep", [(i, (i + X) % groups) for i in range(groups)])
    key_add, val_add = send(key_swap, SWAP), send(val_swap, SWAP)
    context = attend(rotated, key_own, key_add, val_own, val_add, cosine, sine, bias)
    context, rest = tie(context, rest)
    outer_grad = (part.astype(F32) + rest.astype(F32)) / groups
    new_momentum = momentum_coef * momentum + outer_grad
    new_base = outer_base - rate * (outer_grad + momentum_coef * new_momentum)
    return (context, new_base, new_momentum)


def solution(mesh):
    placed = (
        P(("rep", "fsdp"), None),
        P(("rep", "fsdp"), None),
        P(("rep", "fsdp")),
        P("rep", "fsdp", None),
        P("fsdp", None),
        P("fsdp", None),
        P(),
        P(),
    )
    return jax.shard_map(
        body,
        mesh=mesh,
        in_specs=placed,
        out_specs=(P(("rep", "fsdp"), None), P("fsdp", None), P("fsdp", None)),
        check_vma=False,
    )
```

time: 153 us -> 105 us (0.69)
  waiting for transfers between devices: 34.8 us -> 9.82 us
  between operations: 15 us -> 1.58 us
  starting transfers between devices: 35.8 us -> 45.6 us
  Pallas kernels: 44 us -> 35.4 us
  local copies, waits for them, and re-layouts: 12.4 us -> 4.1 us
  other arithmetic: 9.62 us -> 7.57 us
    ppermute x23 -> x24, waiting for transfers between devices: 34.8 us -> 5.09 us  [send(): return lax.ppermute(block, 'fsdp', pairs)]
    unnamed x62 -> x28, local copies, waits for them, and re-layouts: 12 us -> 3.03 us
    ppermute x23 -> x24, starting transfers between devices: 35.2 us -> 40.8 us  [send(): return lax.ppermute(block, 'fsdp', pairs)]
    ppermute x1, waiting for transfers between devices: 0.01 us -> 4.72 us  [body(): lax.ppermute(part, 'rep', [(i, (i + X) % groups) for i in range(groups)])]
    ppermute x0 -> x2, starting transfers between devices: none -> 3.69 us  [the longest x1 2.48 us: body(): rest = lax.ppermute(part, 'rep', along_x(lambda x: X - 1 - x))]
    pallas_call x1, Pallas kernels: 8.47 us -> 4.99 us  [encode(): pl.pallas_call(encode_kernel, out_shape=jax.ShapeDtypeStruct(base.shape,...]
    pallas_call x1, Pallas kernels: 4.44 us -> 1.56 us  [rotate_queries(): pl.pallas_call(rotate_kernel, out_shape=jax.ShapeDtypeStruct(queries.shap...]
    convert_element_type x0 -> x2, other arithmetic: none -> 2.43 us  [add(): return (mine.astype(F32) + theirs.astype(F32)).astype(BF16)]
  transfers between devices with their start and end apart: 25 -> 27, of which waited for: 7 -> 6; matrix products, arithmetic and copies ran while one was open for 4% -> 6% of each run, Pallas kernels for 23% -> 34%
where the time goes in v2:
time: 105 us; the launch traced here: 104 us
  starting transfers between devices  45.6 us (43%)
  Pallas kernels  35.4 us (34%)
  waiting for transfers between devices  9.82 us (9%)
  other arithmetic  7.57 us (7%)
  local copies, waits for them, and re-layouts  4.1 us (4%)
  between operations  1.58 us (2%)
    ppermute x24, starting transfers between devices, send(): return lax.ppermute(block, 'fsdp', pairs)  40.8 us
    pallas_call x4, Pallas kernels, multiply(): pl.pallas_call(functools.partial(multiply_kernel, blocks, moves, spans, n...  19.1 us
    pallas_call x1, Pallas kernels, attend(): pl.pallas_call(attend_kernel, out_shape=jax.ShapeDtypeStruct(rotated.shap...  5.29 us
    ppermute x24, waiting for transfers between devices, send(): return lax.ppermute(block, 'fsdp', pairs)  5.09 us
    pallas_call x1, Pallas kernels, encode(): pl.pallas_call(encode_kernel, out_shape=jax.ShapeDtypeStruct(base.shape,...  4.99 us
    ppermute x1, waiting for transfers between devices, body(): lax.ppermute(part, 'rep', [(i, (i + X) % groups) for i in range(groups)])  4.72 us
    pallas_call x3, Pallas kernels, collect(): pl.pallas_call(functools.partial(collect_kernel, moves, len(sources)), ou...  3.92 us
    unnamed x28, local copies, waits for them, and re-layouts  3.03 us
  transfers between devices with their start and end apart: 27, of which 6 were waited for; matrix products, arithmetic and copies ran while one was open for 6% of the time, Pallas kernels for 34%

profile of v2, /device:TPU:1, one launch (start us, length us, event | category | flops | bytes accessed | tf_op | source)
XLA Modules:
  0.0 104.1 jit_solution(9058550978916407309)
XLA Ops:
  0.6 3.3 %collective-permute-start.3 = (bf16[256,8192]{1,0:T(8,128)(2,1)}, bf16[256,8192]{1,0:T(8,128)(2,1)}, u32[]{:S(2)}, u32[]{:S(2)}) collective-permute-start(bf16[256,8192]{1,0:T(8,128)(2,1)} %refs_0_.7), channel_id=1, source_target_pairs={{0,1},{1,0},{2,3},{3,2},{4,5},{5,4},{6,7},{7,6},{8,9},{9,8},{10,11... | collective-permute-start | bytes 12582920 | tf_op jit(solution)/shard_map/ppermute | solution.py:52
  4.0 3.8 %collective-permute-start.1 = (bf16[256,1024]{1,0:T(8,128)(2,1)}, bf16[256,1024]{1,0:T(8,128)(2,1)S(1)}, u32[]{:S(2)}, u32[]{:S(2)}) collective-permute-start(bf16[256,1024]{1,0:T(8,128)(2,1)} %bitcast.7), channel_id=1, source_target_pairs={{0,28},{1,29},{2,30},{3,31},{4,0},{5,1},{6,2},{7,3},{8,4},{9,5},{1... | collective-permute-start | bytes 1572872 | tf_op jit(solution)/shard_map/ppermute | solution.py:52
  8.9 3.0 %collective-permute-start.2 = (bf16[256,512]{1,0:T(8,128)(2,1)S(1)}, bf16[256,512]{1,0:T(8,128)(2,1)}, u32[]{:S(2)}, u32[]{:S(2)}) collective-permute-start(bf16[256,512]{1,0:T(8,128)(2,1)S(1)} %get-tuple-element.108), channel_id=1, source_target_pairs={{0,2},{1,3},{2,0},{3,1},{4,6},{5,7},{6,4},{7,5},{8,10},{9,11},{10,... | collective-permute-start | bytes 786440 | tf_op jit(solution)/shard_map/ppermute | solution.py:52
  16.8 5.0 %shard_map.103 = bf16[256,1024]{1,0:T(8,128)(2,1)} custom-call(f32[256,1024]{1,0:T(8,128)S(1)} %copy-done.6, bf16[256,1024]{1,0:T(8,128)(2,1)S(1)} %bitcast.11), custom_call_target="tpu_custom_call" | custom-call | tf_op jit(solution)/shard_map/pallas_call | solution.py:374
  22.1 2.7 %collective-permute-start.5 = (bf16[256,1024]{1,0:T(8,128)(2,1)S(1)}, bf16[256,1024]{1,0:T(8,128)(2,1)}, u32[]{:S(2)}, u32[]{:S(2)}) collective-permute-start(bf16[256,1024]{1,0:T(8,128)(2,1)S(1)} %collective-permute-done.1.refs_5_.refs_9_.refs_1_), channel_id=1, source_target_pairs={{0,28},{1,29},{2,30},{3,31},{4,0},{5,1},{6,2},{7,3},{8,4},{9,5},{1... | collective-permute-start | bytes 1572872 | tf_op jit(solution)/shard_map/ppermute | solution.py:52
  25.6 3.0 %collective-permute-start.10 = (bf16[512,512]{1,0:T(8,128)(2,1)}, bf16[512,512]{1,0:T(8,128)(2,1)}, u32[]{:S(2)}, u32[]{:S(2)}) collective-permute-start(bf16[512,512]{1,0:T(8,128)(2,1)} %shard_map.106), channel_id=1, source_target_pairs={{0,2},{1,3},{2,0},{3,1},{4,6},{5,7},{6,4},{7,5},{8,10},{9,11},{10,... | collective-permute-start | bytes 1572872 | tf_op jit(solution)/shard_map/ppermute | solution.py:52
  32.8 4.9 %shard_map.105.refs_8_ = f32[2,512,512]{2,1,0:T(8,128)} custom-call(s32[3]{0:T(128)} %pad_add_fusion.place_ref, bf16[256,8192]{1,0:T(8,128)(2,1)} %refs_0_.7, bf16[256,8192]{1,0:T(8,128)(2,1)} %collective-permute-done.3.refs_1_, bf16[256,1024]{1,0:T(8,128)(2,1)} %bitcast.9, bf16[256,512]{1,0:T(8,128)(2,1)} %collective-permute-done.2.refs_3_, ...), custom_call_target="tpu_custom_call" | custom-call | tf_op jit(solution)/shard_map/pallas_call | solution.py:199
  37.8 2.7 %collective-permute-start.8 = (bf16[256,1024]{1,0:T(8,128)(2,1)}, bf16[256,1024]{1,0:T(8,128)(2,1)S(1)}, u32[]{:S(2)}, u32[]{:S(2)}) collective-permute-start(bf16[256,1024]{1,0:T(8,128)(2,1)} %collective-permute-done.5.refs_4_.refs_7_.refs_1_), channel_id=1, source_target_pairs={{0,28},{1,29},{2,30},{3,31},{4,0},{5,1},{6,2},{7,3},{8,4},{9,5},{1... | collective-permute-start | bytes 1572872 | tf_op jit(solution)/shard_map/ppermute | solution.py:52
  43.3 3.1 %collective-permute-start.16 = (bf16[512,512]{1,0:T(8,128)(2,1)}, bf16[512,512]{1,0:T(8,128)(2,1)}, u32[]{:S(2)}, u32[]{:S(2)}) collective-permute-start(bf16[512,512]{1,0:T(8,128)(2,1)} %shard_map.109), channel_id=1, source_target_pairs={{0,2},{1,3},{2,0},{3,1},{4,6},{5,7},{6,4},{7,5},{8,10},{9,11},{10,... | collective-permute-start | bytes 1572872 | tf_op jit(solution)/shard_map/ppermute | solution.py:52
  46.4 2.7 %collective-permute-start.15 = (bf16[256,512]{1,0:T(8,128)(2,1)}, bf16[256,512]{1,0:T(8,128)(2,1)}, u32[]{:S(2)}, u32[]{:S(2)}) collective-permute-start(bf16[256,512]{1,0:T(8,128)(2,1)} %collective-permute-done.2.refs_3_), channel_id=1, source_target_pairs={{0,28},{1,29},{2,30},{3,31},{4,0},{5,1},{6,2},{7,3},{8,4},{9,5},{1... | collective-permute-start | bytes 786440 | tf_op jit(solution)/shard_map/ppermute | solution.py:52
  49.0 5.1 %shard_map.107.refs_9_ = f32[2,512,512]{2,1,0:T(8,128)} custom-call(s32[3]{0:T(128)} %pad_add_fusion.place_ref, bf16[256,8192]{1,0:T(8,128)(2,1)} %refs_0_.7, bf16[256,8192]{1,0:T(8,128)(2,1)} %collective-permute-done.3.refs_1_, bf16[256,512]{1,0:T(8,128)(2,1)} %collective-permute-done.9.refs_2_, bf16[256,1024]{1,0:T(8,128)(2,1)} %copy-done.3, ...), custom_call_target="tpu_custom_call" | custom-call | tf_op jit(solution)/shard_map/pallas_call | solution.py:199
  54.1 2.2 %add_convert_fusion.1 = bf16[256,1024]{1,0:T(8,128)(2,1)} fusion(bf16[256,1024]{1,0:T(8,128)(2,1)} %collective-permute-done.11, bf16[256,1024]{1,0:T(8,128)(2,1)} %shard_map.103), kind=kLoop, calls=%fused_computation.4 | loop fusion | flops 1048576 | bytes 1572864 | tf_op jit(solution)/shard_map/convert_element_type | solution.py:400
  58.3 2.8 %collective-permute-start.19 = (bf16[512,512]{1,0:T(8,128)(2,1)}, bf16[512,512]{1,0:T(8,128)(2,1)S(1)}, u32[]{:S(2)}, u32[]{:S(2)}) collective-permute-start(bf16[512,512]{1,0:T(8,128)(2,1)} %get-tuple-element.85), channel_id=1, source_target_pairs={{0,2},{1,3},{2,0},{3,1},{4,6},{5,7},{6,4},{7,5},{8,10},{9,11},{10,... | collective-permute-start | bytes 1572872 | tf_op jit(solution)/shard_map/ppermute | solution.py:52
  61.1 2.7 %collective-permute-start.13 = (bf16[256,512]{1,0:T(8,128)(2,1)}, bf16[256,512]{1,0:T(8,128)(2,1)}, u32[]{:S(2)}, u32[]{:S(2)}) collective-permute-start(bf16[256,512]{1,0:T(8,128)(2,1)} %get-tuple-element.74), channel_id=1, source_target_pairs={{0,28},{1,29},{2,30},{3,31},{4,0},{5,1},{6,2},{7,3},{8,4},{9,5},{1... | collective-permute-start | bytes 786440 | tf_op jit(solution)/shard_map/ppermute | solution.py:52
  63.8 2.7 %collective-permute-start.18 = (bf16[256,512]{1,0:T(8,128)(2,1)}, bf16[256,512]{1,0:T(8,128)(2,1)}, u32[]{:S(2)}, u32[]{:S(2)}) collective-permute-start(bf16[256,512]{1,0:T(8,128)(2,1)} %collective-permute-done.15.refs_2_), channel_id=1, source_target_pairs={{0,28},{1,29},{2,30},{3,31},{4,0},{5,1},{6,2},{7,3},{8,4},{9,5},{1... | collective-permute-start | bytes 786440 | tf_op jit(solution)/shard_map/ppermute | solution.py:52
  66.5 5.3 %shard_map.110.refs_7_ = f32[2,512,512]{2,1,0:T(8,128)} custom-call(s32[3]{0:T(128)} %pad_add_fusion.place_ref, bf16[256,8192]{1,0:T(8,128)(2,1)} %refs_0_.7, bf16[256,8192]{1,0:T(8,128)(2,1)} %collective-permute-done.3.refs_1_, bf16[256,512]{1,0:T(8,128)(2,1)} %collective-permute-done.15.refs_2_, bf16[256,512]{1,0:T(8,128)(2,1)} %collective-permute-done.14.refs_3_, ...), custom_call_target="tpu_custom_call" | custom-call | tf_op jit(solution)/shard_map/pallas_call | solution.py:199
  71.8 2.0 %collective-permute-done.17.refs_3_ = bf16[256,512]{1,0:T(8,128)(2,1)} collective-permute-done((bf16[256,512]{1,0:T(8,128)(2,1)}, bf16[256,512]{1,0:T(8,128)(2,1)}, u32[]{:S(2)}, u32[]{:S(2)}) %collective-permute-start.17) | collective-permute-done | bytes 262176 | tf_op jit(solution)/shard_map/ppermute | solution.py:52
  73.8 2.5 %collective-permute-start.20 = (bf16[256,1024]{1,0:T(8,128)(2,1)}, bf16[256,1024]{1,0:T(8,128)(2,1)S(1)}, u32[]{:S(2)}, u32[]{:S(2)}) collective-permute-start(bf16[256,1024]{1,0:T(8,128)(2,1)} %add_convert_fusion.1), channel_id=1, source_target_pairs={{0,96},{32,64},{64,32},{96,0},{128,224},{160,192},{192,160},{224,1... | collective-permute-start | bytes 1572872 | tf_op jit(solution)/shard_map/ppermute | solution.py:488
  76.9 2.7 %collective-permute-start.22 = (bf16[256,512]{1,0:T(8,128)(2,1)}, bf16[256,512]{1,0:T(8,128)(2,1)S(1)}, u32[]{:S(2)}, u32[]{:S(2)}) collective-permute-start(bf16[256,512]{1,0:T(8,128)(2,1)} %collective-permute-done.18.refs_2_), channel_id=1, source_target_pairs={{0,28},{1,29},{2,30},{3,31},{4,0},{5,1},{6,2},{7,3},{8,4},{9,5},{1... | collective-permute-start | bytes 786440 | tf_op jit(solution)/shard_map/ppermute | solution.py:52
  79.6 3.8 %shard_map.111 = (f32[2,512,512]{2,1,0:T(8,128)S(1)}, bf16[512,512]{1,0:T(8,128)(2,1)S(1)}) custom-call(s32[3]{0:T(128)S(1)} %copy-done.9, bf16[256,8192]{1,0:T(8,128)(2,1)} %refs_0_.7, bf16[256,8192]{1,0:T(8,128)(2,1)} %collective-permute-done.3.refs_1_, bf16[256,512]{1,0:T(8,128)(2,1)} %collective-permute-done.18.refs_2_, ...), custom_call_target="tpu_custom_call" | custom-call | tf_op jit(solution)/shard_map/pallas_call | solution.py:199
  84.4 4.4 %collective-permute-start.24 = (f32[256,512]{1,0:T(8,128)S(1)}, f32[256,512]{1,0:T(8,128)S(1)}, u32[]{:S(2)}, u32[]{:S(2)}) collective-permute-start(f32[256,512]{1,0:T(8,128)S(1)} %get-tuple-element.98), channel_id=1, source_target_pairs={{0,1},{1,0},{2,3},{3,2},{4,5},{5,4},{6,7},{7,6},{8,9},{9,8},{10,11... | collective-permute-start | bytes 1572872 | tf_op jit(solution)/shard_map/ppermute | solution.py:52
  91.7 5.3 %shard_map.113 = bf16[256,4096]{1,0:T(8,128)(2,1)} custom-call(bf16[256,4096]{1,0:T(8,128)(2,1)S(1)} %shard_map.104.query_ref, f32[256,512]{1,0:T(8,128)S(1)} %get-tuple-element.97.key_ref, f32[256,512]{1,0:T(8,128)S(1)} %collective-permute-done.24.key_add_ref, f32[256,512]{1,0:T(8,128)S(1)} %get-tuple-element.99.val_ref, ...), custom_call_target="tpu_custom_call" | custom-call | tf_op jit(solution)/shard_map/pallas_call | solution.py:313
  97.0 4.7 %collective-permute-done.26 = bf16[256,1024]{1,0:T(8,128)(2,1)S(1)} collective-permute-done((bf16[256,1024]{1,0:T(8,128)(2,1)S(1)}, bf16[256,1024]{1,0:T(8,128)(2,1)S(1)}, u32[]{:S(2)}, u32[]{:S(2)}) %collective-permute-start.26) | collective-permute-done | bytes 524320 | tf_op jit(solution)/shard_map/ppermute | solution.py:506
  101.7 2.4 %multiply_subtract_fusion = (f32[256,1024]{1,0:T(8,128)}, f32[256,1024]{1,0:T(8,128)}) fusion(f32[256,1024]{1,0:T(8,128)S(1)} %copy-done.7, bf16[256,1024]{1,0:T(8,128)(2,1)S(1)} %collective-permute-done.26, bf16[256,1024]{1,0:T(8,128)(2,1)S(1)} %add_convert_fusion, f32[]{:T(128)} %fusion.4, f32[256,1024]{1,0:T(8,128)S(1)} %copy-done.11), kind=kLoop, calls=%fused_computation | loop fusion | flops 2621440 | bytes 5242884 | tf_op jit(solution)/shard_map/sub | solution.py:512
  (82 shorter events, 19.9 us)
Async XLA Ops:
  0.6 13.9 %collective-permute-start.3 = (bf16[256,8192]{1,0:T(8,128)(2,1)}, bf16[256,8192]{1,0:T(8,128)(2,1)}, u32[]{:S(2)}, u32[]{:S(2)}) collective-permute-start(bf16[256,8192]{1,0:T(8,128)(2,1)} %refs_0_.7), channel_id=1, source_target_pairs={{0,1},{1,0},{2,3},{3,2},{4,5},{5,4},{6,7},{7,6},{8,9},{9,8},{10,11... | collective-permute-start | bytes 12582920 | tf_op jit(solution)/shard_map/ppermute | solution.py:52
  4.0 17.8 %collective-permute-start = (bf16[256,1024]{1,0:T(8,128)(2,1)}, bf16[256,1024]{1,0:T(8,128)(2,1)S(1)}, u32[]{:S(2)}, u32[]{:S(2)}) collective-permute-start(bf16[256,1024]{1,0:T(8,128)(2,1)} %bitcast.6), channel_id=1, source_target_pairs={{0,4},{1,5},{2,6},{3,7},{4,8},{5,9},{6,10},{7,11},{8,12},{9,13},{1... | collective-permute-start | bytes 1572872 | tf_op jit(solution)/shard_map/ppermute | solution.py:52
  4.0 17.8 %collective-permute-start.1 = (bf16[256,1024]{1,0:T(8,128)(2,1)}, bf16[256,1024]{1,0:T(8,128)(2,1)S(1)}, u32[]{:S(2)}, u32[]{:S(2)}) collective-permute-start(bf16[256,1024]{1,0:T(8,128)(2,1)} %bitcast.7), channel_id=1, source_target_pairs={{0,28},{1,29},{2,30},{3,31},{4,0},{5,1},{6,2},{7,3},{8,4},{9,5},{1... | collective-permute-start | bytes 1572872 | tf_op jit(solution)/shard_map/ppermute | solution.py:52
  8.9 12.9 %collective-permute-start.2 = (bf16[256,512]{1,0:T(8,128)(2,1)S(1)}, bf16[256,512]{1,0:T(8,128)(2,1)}, u32[]{:S(2)}, u32[]{:S(2)}) collective-permute-start(bf16[256,512]{1,0:T(8,128)(2,1)S(1)} %get-tuple-element.108), channel_id=1, source_target_pairs={{0,2},{1,3},{2,0},{3,1},{4,6},{5,7},{6,4},{7,5},{8,10},{9,11},{10,... | collective-permute-start | bytes 786440 | tf_op jit(solution)/shard_map/ppermute | solution.py:52
  11.9 17.9 %collective-permute-start.6 = (bf16[256,512]{1,0:T(8,128)(2,1)S(1)}, bf16[256,512]{1,0:T(8,128)(2,1)S(1)}, u32[]{:S(2)}, u32[]{:S(2)}) collective-permute-start(bf16[256,512]{1,0:T(8,128)(2,1)S(1)} %get-tuple-element.107), channel_id=1, source_target_pairs={{0,2},{1,3},{2,0},{3,1},{4,6},{5,7},{6,4},{7,5},{8,10},{9,11},{10,... | collective-permute-start | bytes 786440 | tf_op jit(solution)/shard_map/ppermute | solution.py:52
  22.0 15.7 %collective-permute-start.4 = (bf16[256,1024]{1,0:T(8,128)(2,1)S(1)}, bf16[256,1024]{1,0:T(8,128)(2,1)S(1)}, u32[]{:S(2)}, u32[]{:S(2)}) collective-permute-start(bf16[256,1024]{1,0:T(8,128)(2,1)S(1)} %collective-permute-done.refs_4_.refs_8_.refs_0_), channel_id=1, source_target_pairs={{0,4},{1,5},{2,6},{3,7},{4,8},{5,9},{6,10},{7,11},{8,12},{9,13},{1... | collective-permute-start | bytes 1572872 | tf_op jit(solution)/shard_map/ppermute | solution.py:52
  22.1 15.6 %collective-permute-start.5 = (bf16[256,1024]{1,0:T(8,128)(2,1)S(1)}, bf16[256,1024]{1,0:T(8,128)(2,1)}, u32[]{:S(2)}, u32[]{:S(2)}) collective-permute-start(bf16[256,1024]{1,0:T(8,128)(2,1)S(1)} %collective-permute-done.1.refs_5_.refs_9_.refs_1_), channel_id=1, source_target_pairs={{0,28},{1,29},{2,30},{3,31},{4,0},{5,1},{6,2},{7,3},{8,4},{9,5},{1... | collective-permute-start | bytes 1572872 | tf_op jit(solution)/shard_map/ppermute | solution.py:52
  25.6 15.8 %collective-permute-start.10 = (bf16[512,512]{1,0:T(8,128)(2,1)}, bf16[512,512]{1,0:T(8,128)(2,1)}, u32[]{:S(2)}, u32[]{:S(2)}) collective-permute-start(bf16[512,512]{1,0:T(8,128)(2,1)} %shard_map.106), channel_id=1, source_target_pairs={{0,2},{1,3},{2,0},{3,1},{4,6},{5,7},{6,4},{7,5},{8,10},{9,11},{10,... | collective-permute-start | bytes 1572872 | tf_op jit(solution)/shard_map/ppermute | solution.py:52
  28.5 12.9 %collective-permute-start.11 = (bf16[256,1024]{1,0:T(8,128)(2,1)}, bf16[256,1024]{1,0:T(8,128)(2,1)}, u32[]{:S(2)}, u32[]{:S(2)}) collective-permute-start(bf16[256,1024]{1,0:T(8,128)(2,1)} %shard_map.103), channel_id=1, source_target_pairs={{0,32},{32,0},{64,96},{96,64},{128,160},{160,128},{192,224},{224,1... | collective-permute-start | bytes 1572872 | tf_op jit(solution)/shard_map/ppermute | solution.py:418
  30.5 10.9 %collective-permute-start.9 = (bf16[256,512]{1,0:T(8,128)(2,1)}, bf16[256,512]{1,0:T(8,128)(2,1)}, u32[]{:S(2)}, u32[]{:S(2)}) collective-permute-start(bf16[256,512]{1,0:T(8,128)(2,1)} %collective-permute-done.2.refs_3_), channel_id=1, source_target_pairs={{0,4},{1,5},{2,6},{3,7},{4,8},{5,9},{6,10},{7,11},{8,12},{9,13},{1... | collective-permute-start | bytes 786440 | tf_op jit(solution)/shard_map/ppermute | solution.py:52
  37.7 18.7 %collective-permute-start.7 = (bf16[256,1024]{1,0:T(8,128)(2,1)S(1)}, bf16[256,1024]{1,0:T(8,128)(2,1)S(1)}, u32[]{:S(2)}, u32[]{:S(2)}) collective-permute-start(bf16[256,1024]{1,0:T(8,128)(2,1)S(1)} %collective-permute-done.4.refs_3_.refs_6_.refs_0_), channel_id=1, source_target_pairs={{0,4},{1,5},{2,6},{3,7},{4,8},{5,9},{6,10},{7,11},{8,12},{9,13},{1... | collective-permute-start | bytes 1572872 | tf_op jit(solution)/shard_map/ppermute | solution.py:52
  37.8 18.5 %collective-permute-start.8 = (bf16[256,1024]{1,0:T(8,128)(2,1)}, bf16[256,1024]{1,0:T(8,128)(2,1)S(1)}, u32[]{:S(2)}, u32[]{:S(2)}) collective-permute-start(bf16[256,1024]{1,0:T(8,128)(2,1)} %collective-permute-done.5.refs_4_.refs_7_.refs_1_), channel_id=1, source_target_pairs={{0,28},{1,29},{2,30},{3,31},{4,0},{5,1},{6,2},{7,3},{8,4},{9,5},{1... | collective-permute-start | bytes 1572872 | tf_op jit(solution)/shard_map/ppermute | solution.py:52
  43.3 15.0 %collective-permute-start.16 = (bf16[512,512]{1,0:T(8,128)(2,1)}, bf16[512,512]{1,0:T(8,128)(2,1)}, u32[]{:S(2)}, u32[]{:S(2)}) collective-permute-start(bf16[512,512]{1,0:T(8,128)(2,1)} %shard_map.109), channel_id=1, source_target_pairs={{0,2},{1,3},{2,0},{3,1},{4,6},{5,7},{6,4},{7,5},{8,10},{9,11},{10,... | collective-permute-start | bytes 1572872 | tf_op jit(solution)/shard_map/ppermute | solution.py:52
  46.4 11.9 %collective-permute-start.14 = (bf16[256,512]{1,0:T(8,128)(2,1)}, bf16[256,512]{1,0:T(8,128)(2,1)}, u32[]{:S(2)}, u32[]{:S(2)}) collective-permute-start(bf16[256,512]{1,0:T(8,128)(2,1)} %collective-permute-done.9.refs_2_), channel_id=1, source_target_pairs={{0,4},{1,5},{2,6},{3,7},{4,8},{5,9},{6,10},{7,11},{8,12},{9,13},{1... | collective-permute-start | bytes 786440 | tf_op jit(solution)/shard_map/ppermute | solution.py:52
  46.4 11.9 %collective-permute-start.15 = (bf16[256,512]{1,0:T(8,128)(2,1)}, bf16[256,512]{1,0:T(8,128)(2,1)}, u32[]{:S(2)}, u32[]{:S(2)}) collective-permute-start(bf16[256,512]{1,0:T(8,128)(2,1)} %collective-permute-done.2.refs_3_), channel_id=1, source_target_pairs={{0,28},{1,29},{2,30},{3,31},{4,0},{5,1},{6,2},{7,3},{8,4},{9,5},{1... | collective-permute-start | bytes 786440 | tf_op jit(solution)/shard_map/ppermute | solution.py:52
  58.3 15.5 %collective-permute-start.19 = (bf16[512,512]{1,0:T(8,128)(2,1)}, bf16[512,512]{1,0:T(8,128)(2,1)S(1)}, u32[]{:S(2)}, u32[]{:S(2)}) collective-permute-start(bf16[512,512]{1,0:T(8,128)(2,1)} %get-tuple-element.85), channel_id=1, source_target_pairs={{0,2},{1,3},{2,0},{3,1},{4,6},{5,7},{6,4},{7,5},{8,10},{9,11},{10,... | collective-permute-start | bytes 1572872 | tf_op jit(solution)/shard_map/ppermute | solution.py:52
  61.1 10.7 %collective-permute-start.12 = (bf16[256,512]{1,0:T(8,128)(2,1)}, bf16[256,512]{1,0:T(8,128)(2,1)}, u32[]{:S(2)}, u32[]{:S(2)}) collective-permute-start(bf16[256,512]{1,0:T(8,128)(2,1)} %get-tuple-element.73), channel_id=1, source_target_pairs={{0,4},{1,5},{2,6},{3,7},{4,8},{5,9},{6,10},{7,11},{8,12},{9,13},{1... | collective-permute-start | bytes 786440 | tf_op jit(solution)/shard_map/ppermute | solution.py:52
  61.1 10.7 %collective-permute-start.13 = (bf16[256,512]{1,0:T(8,128)(2,1)}, bf16[256,512]{1,0:T(8,128)(2,1)}, u32[]{:S(2)}, u32[]{:S(2)}) collective-permute-start(bf16[256,512]{1,0:T(8,128)(2,1)} %get-tuple-element.74), channel_id=1, source_target_pairs={{0,28},{1,29},{2,30},{3,31},{4,0},{5,1},{6,2},{7,3},{8,4},{9,5},{1... | collective-permute-start | bytes 786440 | tf_op jit(solution)/shard_map/ppermute | solution.py:52
  63.8 10.0 %collective-permute-start.17 = (bf16[256,512]{1,0:T(8,128)(2,1)}, bf16[256,512]{1,0:T(8,128)(2,1)}, u32[]{:S(2)}, u32[]{:S(2)}) collective-permute-start(bf16[256,512]{1,0:T(8,128)(2,1)} %collective-permute-done.14.refs_3_), channel_id=1, source_target_pairs={{0,4},{1,5},{2,6},{3,7},{4,8},{5,9},{6,10},{7,11},{8,12},{9,13},{1... | collective-permute-start | bytes 786440 | tf_op jit(solution)/shard_map/ppermute | solution.py:52
  63.8 10.0 %collective-permute-start.18 = (bf16[256,512]{1,0:T(8,128)(2,1)}, bf16[256,512]{1,0:T(8,128)(2,1)}, u32[]{:S(2)}, u32[]{:S(2)}) collective-permute-start(bf16[256,512]{1,0:T(8,128)(2,1)} %collective-permute-done.15.refs_2_), channel_id=1, source_target_pairs={{0,28},{1,29},{2,30},{3,31},{4,0},{5,1},{6,2},{7,3},{8,4},{9,5},{1... | collective-permute-start | bytes 786440 | tf_op jit(solution)/shard_map/ppermute | solution.py:52
  73.8 15.0 %collective-permute-start.20 = (bf16[256,1024]{1,0:T(8,128)(2,1)}, bf16[256,1024]{1,0:T(8,128)(2,1)S(1)}, u32[]{:S(2)}, u32[]{:S(2)}) collective-permute-start(bf16[256,1024]{1,0:T(8,128)(2,1)} %add_convert_fusion.1), channel_id=1, source_target_pairs={{0,96},{32,64},{64,32},{96,0},{128,224},{160,192},{192,160},{224,1... | collective-permute-start | bytes 1572872 | tf_op jit(solution)/shard_map/ppermute | solution.py:488
  76.3 7.1 %collective-permute-start.23 = (bf16[256,512]{1,0:T(8,128)(2,1)}, bf16[256,512]{1,0:T(8,128)(2,1)S(1)}, u32[]{:S(2)}, u32[]{:S(2)}) collective-permute-start(bf16[256,512]{1,0:T(8,128)(2,1)} %collective-permute-done.12.refs_6_), channel_id=1, source_target_pairs={{0,2},{1,3},{2,0},{3,1},{4,6},{5,7},{6,4},{7,5},{8,10},{9,11},{10,... | collective-permute-start | bytes 786440 | tf_op jit(solution)/shard_map/ppermute | solution.py:52
  84.4 7.3 %collective-permute-start.24 = (f32[256,512]{1,0:T(8,128)S(1)}, f32[256,512]{1,0:T(8,128)S(1)}, u32[]{:S(2)}, u32[]{:S(2)}) collective-permute-start(f32[256,512]{1,0:T(8,128)S(1)} %get-tuple-element.98), channel_id=1, source_target_pairs={{0,1},{1,0},{2,3},{3,2},{4,5},{5,4},{6,7},{7,6},{8,9},{9,8},{10,11... | collective-permute-start | bytes 1572872 | tf_op jit(solution)/shard_map/ppermute | solution.py:52
  89.0 12.7 %collective-permute-start.26 = (bf16[256,1024]{1,0:T(8,128)(2,1)S(1)}, bf16[256,1024]{1,0:T(8,128)(2,1)S(1)}, u32[]{:S(2)}, u32[]{:S(2)}) collective-permute-start(bf16[256,1024]{1,0:T(8,128)(2,1)S(1)} %add_convert_fusion), channel_id=1, source_target_pairs={{0,128},{32,160},{64,192},{96,224},{128,0},{160,32},{192,64},{224,... | collective-permute-start | bytes 1572872 | tf_op jit(solution)/shard_map/ppermute | solution.py:506
  (17 other events, 151.4 us)

commit v3 on v2

--- a/solution.py
+++ b/solution.py
@@ -378,7 +378,7 @@
         in_specs=[spec, spec],
         out_specs=spec,
         cost_estimate=NO_COST,
-        compiler_params=pltpu.CompilerParams(vmem_limit_bytes=6 * 2**20),
+        compiler_params=pltpu.CompilerParams(vmem_limit_bytes=56 * 2**20),
     )(base, weights)
 
 

time: 105 us -> 104 us (level)
  local copies, waits for them, and re-layouts: 4.1 us -> 1.11 us
  Pallas kernels: 35.4 us -> 36.7 us
    unnamed x28 -> x24, local copies, waits for them, and re-layouts: 3.03 us -> 0.05 us
    pallas_call x1, Pallas kernels: 4.99 us -> 6.26 us  [encode(): pl.pallas_call(encode_kernel, out_shape=jax.ShapeDtypeStruct(base.shape,...]
  transfers between devices with their start and end apart: 27 -> 27, of which waited for: 6 -> 6; matrix products, arithmetic and copies ran while one was open for 6% -> 6% of each run, Pallas kernels for 34% -> 36%
where the time goes in v3:
time: 104 us; the launch traced here: 103 us
  starting transfers between devices  45.7 us (44%)
  Pallas kernels  36.7 us (35%)
  waiting for transfers between devices  10.5 us (10%)
  other arithmetic  7.61 us (7%)
  between operations  1.6 us (2%)
  local copies, waits for them, and re-layouts  1.11 us (1%)
    ppermute x24, starting transfers between devices, send(): return lax.ppermute(block, 'fsdp', pairs)  40.9 us
    pallas_call x4, Pallas kernels, multiply(): pl.pallas_call(functools.partial(multiply_kernel, blocks, moves, spans, n...  19.1 us
    pallas_call x1, Pallas kernels, encode(): pl.pallas_call(encode_kernel, out_shape=jax.ShapeDtypeStruct(base.shape,...  6.26 us
    ppermute x24, waiting for transfers between devices, send(): return lax.ppermute(block, 'fsdp', pairs)  5.74 us
    pallas_call x1, Pallas kernels, attend(): pl.pallas_call(attend_kernel, out_shape=jax.ShapeDtypeStruct(rotated.shap...  5.29 us
    ppermute x1, waiting for transfers between devices, body(): lax.ppermute(part, 'rep', [(i, (i + X) % groups) for i in range(groups)])  4.71 us
    pallas_call x3, Pallas kernels, collect(): pl.pallas_call(functools.partial(collect_kernel, moves, len(sources)), ou...  3.91 us
    ppermute x1, starting transfers between devices, body(): rest = lax.ppermute(part, 'rep', along_x(lambda x: X - 1 - x))  2.48 us
  transfers between devices with their start and end apart: 27, of which 6 were waited for; matrix products, arithmetic and copies ran while one was open for 6% of the time, Pallas kernels for 36%

profile of v3, /device:TPU:1, one launch (start us, length us, event | category | flops | bytes accessed | tf_op | source)
XLA Modules:
  0.0 103.1 jit_solution(2017812165631100441)
XLA Ops:
  0.6 3.3 %collective-permute-start.3 = (bf16[256,8192]{1,0:T(8,128)(2,1)}, bf16[256,8192]{1,0:T(8,128)(2,1)}, u32[]{:S(2)}, u32[]{:S(2)}) collective-permute-start(bf16[256,8192]{1,0:T(8,128)(2,1)} %refs_0_.7), channel_id=1, source_target_pairs={{0,1},{1,0},{2,3},{3,2},{4,5},{5,4},{6,7},{7,6},{8,9},{9,8},{10,11... | collective-permute-start | bytes 12582920 | tf_op jit(solution)/shard_map/ppermute | solution.py:52
  4.0 3.8 %collective-permute-start.1 = (bf16[256,1024]{1,0:T(8,128)(2,1)}, bf16[256,1024]{1,0:T(8,128)(2,1)S(1)}, u32[]{:S(2)}, u32[]{:S(2)}) collective-permute-start(bf16[256,1024]{1,0:T(8,128)(2,1)} %bitcast.7), channel_id=1, source_target_pairs={{0,28},{1,29},{2,30},{3,31},{4,0},{5,1},{6,2},{7,3},{8,4},{9,5},{1... | collective-permute-start | bytes 1572872 | tf_op jit(solution)/shard_map/ppermute | solution.py:52
  8.9 3.0 %collective-permute-start.2 = (bf16[256,512]{1,0:T(8,128)(2,1)S(1)}, bf16[256,512]{1,0:T(8,128)(2,1)}, u32[]{:S(2)}, u32[]{:S(2)}) collective-permute-start(bf16[256,512]{1,0:T(8,128)(2,1)S(1)} %get-tuple-element.108), channel_id=1, source_target_pairs={{0,2},{1,3},{2,0},{3,1},{4,6},{5,7},{6,4},{7,5},{8,10},{9,11},{10,... | collective-permute-start | bytes 786440 | tf_op jit(solution)/shard_map/ppermute | solution.py:52
  14.6 6.3 %shard_map.103 = bf16[256,1024]{1,0:T(8,128)(2,1)} custom-call(f32[256,1024]{1,0:T(8,128)} %base_ref.1, bf16[256,1024]{1,0:T(8,128)(2,1)} %bitcast.9), custom_call_target="tpu_custom_call" | custom-call | tf_op jit(solution)/shard_map/pallas_call | solution.py:374
  21.1 2.7 %collective-permute-start.5 = (bf16[256,1024]{1,0:T(8,128)(2,1)S(1)}, bf16[256,1024]{1,0:T(8,128)(2,1)}, u32[]{:S(2)}, u32[]{:S(2)}) collective-permute-start(bf16[256,1024]{1,0:T(8,128)(2,1)S(1)} %collective-permute-done.1.refs_5_.refs_9_.refs_1_), channel_id=1, source_target_pairs={{0,28},{1,29},{2,30},{3,31},{4,0},{5,1},{6,2},{7,3},{8,4},{9,5},{1... | collective-permute-start | bytes 1572872 | tf_op jit(solution)/shard_map/ppermute | solution.py:52
  24.6 3.0 %collective-permute-start.10 = (bf16[512,512]{1,0:T(8,128)(2,1)}, bf16[512,512]{1,0:T(8,128)(2,1)}, u32[]{:S(2)}, u32[]{:S(2)}) collective-permute-start(bf16[512,512]{1,0:T(8,128)(2,1)} %shard_map.106), channel_id=1, source_target_pairs={{0,2},{1,3},{2,0},{3,1},{4,6},{5,7},{6,4},{7,5},{8,10},{9,11},{10,... | collective-permute-start | bytes 1572872 | tf_op jit(solution)/shard_map/ppermute | solution.py:52
  31.2 4.9 %shard_map.105.refs_8_ = f32[2,512,512]{2,1,0:T(8,128)} custom-call(s32[3]{0:T(128)} %pad_add_fusion.place_ref, bf16[256,8192]{1,0:T(8,128)(2,1)} %refs_0_.7, bf16[256,8192]{1,0:T(8,128)(2,1)} %collective-permute-done.3.refs_1_, bf16[256,1024]{1,0:T(8,128)(2,1)} %bitcast.10, bf16[256,512]{1,0:T(8,128)(2,1)} %collective-permute-done.2.refs_3_, ...), custom_call_target="tpu_custom_call" | custom-call | tf_op jit(solution)/shard_map/pallas_call | solution.py:199
  40.5 1.8 %shard_map.109 = bf16[512,512]{1,0:T(8,128)(2,1)} custom-call(bf16[256,1024]{1,0:T(8,128)(2,1)S(1)} %collective-permute-done.4.refs_3_.refs_6_.refs_0_, bf16[256,1024]{1,0:T(8,128)(2,1)} %collective-permute-done.5.refs_4_.refs_7_.refs_1_), custom_call_target="tpu_custom_call" | custom-call | tf_op jit(solution)/shard_map/pallas_call | solution.py:80
  42.3 3.1 %collective-permute-start.16 = (bf16[512,512]{1,0:T(8,128)(2,1)}, bf16[512,512]{1,0:T(8,128)(2,1)}, u32[]{:S(2)}, u32[]{:S(2)}) collective-permute-start(bf16[512,512]{1,0:T(8,128)(2,1)} %shard_map.109), channel_id=1, source_target_pairs={{0,2},{1,3},{2,0},{3,1},{4,6},{5,7},{6,4},{7,5},{8,10},{9,11},{10,... | collective-permute-start | bytes 1572872 | tf_op jit(solution)/shard_map/ppermute | solution.py:52
  45.4 2.7 %collective-permute-start.15 = (bf16[256,512]{1,0:T(8,128)(2,1)}, bf16[256,512]{1,0:T(8,128)(2,1)}, u32[]{:S(2)}, u32[]{:S(2)}) collective-permute-start(bf16[256,512]{1,0:T(8,128)(2,1)} %collective-permute-done.2.refs_3_), channel_id=1, source_target_pairs={{0,28},{1,29},{2,30},{3,31},{4,0},{5,1},{6,2},{7,3},{8,4},{9,5},{1... | collective-permute-start | bytes 786440 | tf_op jit(solution)/shard_map/ppermute | solution.py:52
  48.1 5.1 %shard_map.107.refs_9_ = f32[2,512,512]{2,1,0:T(8,128)} custom-call(s32[3]{0:T(128)} %pad_add_fusion.place_ref, bf16[256,8192]{1,0:T(8,128)(2,1)} %refs_0_.7, bf16[256,8192]{1,0:T(8,128)(2,1)} %collective-permute-done.3.refs_1_, bf16[256,512]{1,0:T(8,128)(2,1)} %collective-permute-done.9.refs_2_, bf16[256,1024]{1,0:T(8,128)(2,1)} %copy-done.2, ...), custom_call_target="tpu_custom_call" | custom-call | tf_op jit(solution)/shard_map/pallas_call | solution.py:199
  53.2 2.2 %add_convert_fusion.1 = bf16[256,1024]{1,0:T(8,128)(2,1)} fusion(bf16[256,1024]{1,0:T(8,128)(2,1)} %collective-permute-done.11, bf16[256,1024]{1,0:T(8,128)(2,1)} %shard_map.103), kind=kLoop, calls=%fused_computation.4 | loop fusion | flops 1048576 | bytes 1572864 | tf_op jit(solution)/shard_map/convert_element_type | solution.py:400
  57.3 2.8 %collective-permute-start.19 = (bf16[512,512]{1,0:T(8,128)(2,1)}, bf16[512,512]{1,0:T(8,128)(2,1)S(1)}, u32[]{:S(2)}, u32[]{:S(2)}) collective-permute-start(bf16[512,512]{1,0:T(8,128)(2,1)} %get-tuple-element.85), channel_id=1, source_target_pairs={{0,2},{1,3},{2,0},{3,1},{4,6},{5,7},{6,4},{7,5},{8,10},{9,11},{10,... | collective-permute-start | bytes 1572872 | tf_op jit(solution)/shard_map/ppermute | solution.py:52
  60.2 2.7 %collective-permute-start.13 = (bf16[256,512]{1,0:T(8,128)(2,1)}, bf16[256,512]{1,0:T(8,128)(2,1)}, u32[]{:S(2)}, u32[]{:S(2)}) collective-permute-start(bf16[256,512]{1,0:T(8,128)(2,1)} %get-tuple-element.74), channel_id=1, source_target_pairs={{0,28},{1,29},{2,30},{3,31},{4,0},{5,1},{6,2},{7,3},{8,4},{9,5},{1... | collective-permute-start | bytes 786440 | tf_op jit(solution)/shard_map/ppermute | solution.py:52
  62.8 2.7 %collective-permute-start.18 = (bf16[256,512]{1,0:T(8,128)(2,1)}, bf16[256,512]{1,0:T(8,128)(2,1)}, u32[]{:S(2)}, u32[]{:S(2)}) collective-permute-start(bf16[256,512]{1,0:T(8,128)(2,1)} %collective-permute-done.15.refs_2_), channel_id=1, source_target_pairs={{0,28},{1,29},{2,30},{3,31},{4,0},{5,1},{6,2},{7,3},{8,4},{9,5},{1... | collective-permute-start | bytes 786440 | tf_op jit(solution)/shard_map/ppermute | solution.py:52
  65.5 5.3 %shard_map.110.refs_7_ = f32[2,512,512]{2,1,0:T(8,128)} custom-call(s32[3]{0:T(128)} %pad_add_fusion.place_ref, bf16[256,8192]{1,0:T(8,128)(2,1)} %refs_0_.7, bf16[256,8192]{1,0:T(8,128)(2,1)} %collective-permute-done.3.refs_1_, bf16[256,512]{1,0:T(8,128)(2,1)} %collective-permute-done.15.refs_2_, bf16[256,512]{1,0:T(8,128)(2,1)} %collective-permute-done.14.refs_3_, ...), custom_call_target="tpu_custom_call" | custom-call | tf_op jit(solution)/shard_map/pallas_call | solution.py:199
  70.9 2.0 %collective-permute-done.17.refs_3_ = bf16[256,512]{1,0:T(8,128)(2,1)} collective-permute-done((bf16[256,512]{1,0:T(8,128)(2,1)}, bf16[256,512]{1,0:T(8,128)(2,1)}, u32[]{:S(2)}, u32[]{:S(2)}) %collective-permute-start.17) | collective-permute-done | bytes 262176 | tf_op jit(solution)/shard_map/ppermute | solution.py:52
  72.9 2.5 %collective-permute-start.20 = (bf16[256,1024]{1,0:T(8,128)(2,1)}, bf16[256,1024]{1,0:T(8,128)(2,1)S(1)}, u32[]{:S(2)}, u32[]{:S(2)}) collective-permute-start(bf16[256,1024]{1,0:T(8,128)(2,1)} %add_convert_fusion.1), channel_id=1, source_target_pairs={{0,96},{32,64},{64,32},{96,0},{128,224},{160,192},{192,160},{224,1... | collective-permute-start | bytes 1572872 | tf_op jit(solution)/shard_map/ppermute | solution.py:488
  75.9 2.7 %collective-permute-start.22 = (bf16[256,512]{1,0:T(8,128)(2,1)}, bf16[256,512]{1,0:T(8,128)(2,1)S(1)}, u32[]{:S(2)}, u32[]{:S(2)}) collective-permute-start(bf16[256,512]{1,0:T(8,128)(2,1)} %collective-permute-done.18.refs_2_), channel_id=1, source_target_pairs={{0,28},{1,29},{2,30},{3,31},{4,0},{5,1},{6,2},{7,3},{8,4},{9,5},{1... | collective-permute-start | bytes 786440 | tf_op jit(solution)/shard_map/ppermute | solution.py:52
  78.6 3.8 %shard_map.111 = (f32[2,512,512]{2,1,0:T(8,128)S(1)}, bf16[512,512]{1,0:T(8,128)(2,1)S(1)}) custom-call(s32[3]{0:T(128)S(1)} %copy-done.6, bf16[256,8192]{1,0:T(8,128)(2,1)} %refs_0_.7, bf16[256,8192]{1,0:T(8,128)(2,1)} %collective-permute-done.3.refs_1_, bf16[256,512]{1,0:T(8,128)(2,1)} %collective-permute-done.18.refs_2_, ...), custom_call_target="tpu_custom_call" | custom-call | tf_op jit(solution)/shard_map/pallas_call | solution.py:199
  83.4 4.4 %collective-permute-start.24 = (f32[256,512]{1,0:T(8,128)S(1)}, f32[256,512]{1,0:T(8,128)S(1)}, u32[]{:S(2)}, u32[]{:S(2)}) collective-permute-start(f32[256,512]{1,0:T(8,128)S(1)} %get-tuple-element.98), channel_id=1, source_target_pairs={{0,1},{1,0},{2,3},{3,2},{4,5},{5,4},{6,7},{7,6},{8,9},{9,8},{10,11... | collective-permute-start | bytes 1572872 | tf_op jit(solution)/shard_map/ppermute | solution.py:52
  90.8 5.3 %shard_map.113 = bf16[256,4096]{1,0:T(8,128)(2,1)} custom-call(bf16[256,4096]{1,0:T(8,128)(2,1)S(1)} %shard_map.104.query_ref, f32[256,512]{1,0:T(8,128)S(1)} %get-tuple-element.97.key_ref, f32[256,512]{1,0:T(8,128)S(1)} %collective-permute-done.24.key_add_ref, f32[256,512]{1,0:T(8,128)S(1)} %get-tuple-element.99.val_ref, ...), custom_call_target="tpu_custom_call" | custom-call | tf_op jit(solution)/shard_map/pallas_call | solution.py:313
  96.1 4.7 %collective-permute-done.26 = bf16[256,1024]{1,0:T(8,128)(2,1)S(1)} collective-permute-done((bf16[256,1024]{1,0:T(8,128)(2,1)S(1)}, bf16[256,1024]{1,0:T(8,128)(2,1)S(1)}, u32[]{:S(2)}, u32[]{:S(2)}) %collective-permute-start.26) | collective-permute-done | bytes 524320 | tf_op jit(solution)/shard_map/ppermute | solution.py:506
  100.8 2.4 %multiply_subtract_fusion = (f32[256,1024]{1,0:T(8,128)}, f32[256,1024]{1,0:T(8,128)}) fusion(f32[256,1024]{1,0:T(8,128)S(1)} %copy-done.7, bf16[256,1024]{1,0:T(8,128)(2,1)S(1)} %collective-permute-done.26, bf16[256,1024]{1,0:T(8,128)(2,1)S(1)} %add_convert_fusion, f32[]{:T(128)} %fusion.4, f32[256,1024]{1,0:T(8,128)S(1)} %copy-done.9), kind=kLoop, calls=%fused_computation | loop fusion | flops 2621440 | bytes 5242884 | tf_op jit(solution)/shard_map/sub | solution.py:512
  (78 shorter events, 18.5 us)
Async XLA Ops:
  0.6 13.9 %collective-permute-start.3 = (bf16[256,8192]{1,0:T(8,128)(2,1)}, bf16[256,8192]{1,0:T(8,128)(2,1)}, u32[]{:S(2)}, u32[]{:S(2)}) collective-permute-start(bf16[256,8192]{1,0:T(8,128)(2,1)} %refs_0_.7), channel_id=1, source_target_pairs={{0,1},{1,0},{2,3},{3,2},{4,5},{5,4},{6,7},{7,6},{8,9},{9,8},{10,11... | collective-permute-start | bytes 12582920 | tf_op jit(solution)/shard_map/ppermute | solution.py:52
  4.0 16.9 %collective-permute-start = (bf16[256,1024]{1,0:T(8,128)(2,1)}, bf16[256,1024]{1,0:T(8,128)(2,1)S(1)}, u32[]{:S(2)}, u32[]{:S(2)}) collective-permute-start(bf16[256,1024]{1,0:T(8,128)(2,1)} %bitcast.6), channel_id=1, source_target_pairs={{0,4},{1,5},{2,6},{3,7},{4,8},{5,9},{6,10},{7,11},{8,12},{9,13},{1... | collective-permute-start | bytes 1572872 | tf_op jit(solution)/shard_map/ppermute | solution.py:52
  4.0 16.9 %collective-permute-start.1 = (bf16[256,1024]{1,0:T(8,128)(2,1)}, bf16[256,1024]{1,0:T(8,128)(2,1)S(1)}, u32[]{:S(2)}, u32[]{:S(2)}) collective-permute-start(bf16[256,1024]{1,0:T(8,128)(2,1)} %bitcast.7), channel_id=1, source_target_pairs={{0,28},{1,29},{2,30},{3,31},{4,0},{5,1},{6,2},{7,3},{8,4},{9,5},{1... | collective-permute-start | bytes 1572872 | tf_op jit(solution)/shard_map/ppermute | solution.py:52
  8.9 12.0 %collective-permute-start.2 = (bf16[256,512]{1,0:T(8,128)(2,1)S(1)}, bf16[256,512]{1,0:T(8,128)(2,1)}, u32[]{:S(2)}, u32[]{:S(2)}) collective-permute-start(bf16[256,512]{1,0:T(8,128)(2,1)S(1)} %get-tuple-element.108), channel_id=1, source_target_pairs={{0,2},{1,3},{2,0},{3,1},{4,6},{5,7},{6,4},{7,5},{8,10},{9,11},{10,... | collective-permute-start | bytes 786440 | tf_op jit(solution)/shard_map/ppermute | solution.py:52
  11.9 16.9 %collective-permute-start.6 = (bf16[256,512]{1,0:T(8,128)(2,1)S(1)}, bf16[256,512]{1,0:T(8,128)(2,1)S(1)}, u32[]{:S(2)}, u32[]{:S(2)}) collective-permute-start(bf16[256,512]{1,0:T(8,128)(2,1)S(1)} %get-tuple-element.107), channel_id=1, source_target_pairs={{0,2},{1,3},{2,0},{3,1},{4,6},{5,7},{6,4},{7,5},{8,10},{9,11},{10,... | collective-permute-start | bytes 786440 | tf_op jit(solution)/shard_map/ppermute | solution.py:52
  21.0 15.0 %collective-permute-start.4 = (bf16[256,1024]{1,0:T(8,128)(2,1)S(1)}, bf16[256,1024]{1,0:T(8,128)(2,1)S(1)}, u32[]{:S(2)}, u32[]{:S(2)}) collective-permute-start(bf16[256,1024]{1,0:T(8,128)(2,1)S(1)} %collective-permute-done.refs_4_.refs_8_.refs_0_), channel_id=1, source_target_pairs={{0,4},{1,5},{2,6},{3,7},{4,8},{5,9},{6,10},{7,11},{8,12},{9,13},{1... | collective-permute-start | bytes 1572872 | tf_op jit(solution)/shard_map/ppermute | solution.py:52
  21.1 15.0 %collective-permute-start.5 = (bf16[256,1024]{1,0:T(8,128)(2,1)S(1)}, bf16[256,1024]{1,0:T(8,128)(2,1)}, u32[]{:S(2)}, u32[]{:S(2)}) collective-permute-start(bf16[256,1024]{1,0:T(8,128)(2,1)S(1)} %collective-permute-done.1.refs_5_.refs_9_.refs_1_), channel_id=1, source_target_pairs={{0,28},{1,29},{2,30},{3,31},{4,0},{5,1},{6,2},{7,3},{8,4},{9,5},{1... | collective-permute-start | bytes 1572872 | tf_op jit(solution)/shard_map/ppermute | solution.py:52
  24.6 15.8 %collective-permute-start.10 = (bf16[512,512]{1,0:T(8,128)(2,1)}, bf16[512,512]{1,0:T(8,128)(2,1)}, u32[]{:S(2)}, u32[]{:S(2)}) collective-permute-start(bf16[512,512]{1,0:T(8,128)(2,1)} %shard_map.106), channel_id=1, source_target_pairs={{0,2},{1,3},{2,0},{3,1},{4,6},{5,7},{6,4},{7,5},{8,10},{9,11},{10,... | collective-permute-start | bytes 1572872 | tf_op jit(solution)/shard_map/ppermute | solution.py:52
  27.6 12.9 %collective-permute-start.11 = (bf16[256,1024]{1,0:T(8,128)(2,1)}, bf16[256,1024]{1,0:T(8,128)(2,1)}, u32[]{:S(2)}, u32[]{:S(2)}) collective-permute-start(bf16[256,1024]{1,0:T(8,128)(2,1)} %shard_map.103), channel_id=1, source_target_pairs={{0,32},{32,0},{64,96},{96,64},{128,160},{160,128},{192,224},{224,1... | collective-permute-start | bytes 1572872 | tf_op jit(solution)/shard_map/ppermute | solution.py:418
  28.8 11.7 %collective-permute-start.9 = (bf16[256,512]{1,0:T(8,128)(2,1)}, bf16[256,512]{1,0:T(8,128)(2,1)}, u32[]{:S(2)}, u32[]{:S(2)}) collective-permute-start(bf16[256,512]{1,0:T(8,128)(2,1)} %collective-permute-done.2.refs_3_), channel_id=1, source_target_pairs={{0,4},{1,5},{2,6},{3,7},{4,8},{5,9},{6,10},{7,11},{8,12},{9,13},{1... | collective-permute-start | bytes 786440 | tf_op jit(solution)/shard_map/ppermute | solution.py:52
  36.1 19.3 %collective-permute-start.7 = (bf16[256,1024]{1,0:T(8,128)(2,1)S(1)}, bf16[256,1024]{1,0:T(8,128)(2,1)S(1)}, u32[]{:S(2)}, u32[]{:S(2)}) collective-permute-start(bf16[256,1024]{1,0:T(8,128)(2,1)S(1)} %collective-permute-done.4.refs_3_.refs_6_.refs_0_), channel_id=1, source_target_pairs={{0,4},{1,5},{2,6},{3,7},{4,8},{5,9},{6,10},{7,11},{8,12},{9,13},{1... | collective-permute-start | bytes 1572872 | tf_op jit(solution)/shard_map/ppermute | solution.py:52
  37.2 18.2 %collective-permute-start.8 = (bf16[256,1024]{1,0:T(8,128)(2,1)}, bf16[256,1024]{1,0:T(8,128)(2,1)S(1)}, u32[]{:S(2)}, u32[]{:S(2)}) collective-permute-start(bf16[256,1024]{1,0:T(8,128)(2,1)} %collective-permute-done.5.refs_4_.refs_7_.refs_1_), channel_id=1, source_target_pairs={{0,28},{1,29},{2,30},{3,31},{4,0},{5,1},{6,2},{7,3},{8,4},{9,5},{1... | collective-permute-start | bytes 1572872 | tf_op jit(solution)/shard_map/ppermute | solution.py:52
  42.3 15.0 %collective-permute-start.16 = (bf16[512,512]{1,0:T(8,128)(2,1)}, bf16[512,512]{1,0:T(8,128)(2,1)}, u32[]{:S(2)}, u32[]{:S(2)}) collective-permute-start(bf16[512,512]{1,0:T(8,128)(2,1)} %shard_map.109), channel_id=1, source_target_pairs={{0,2},{1,3},{2,0},{3,1},{4,6},{5,7},{6,4},{7,5},{8,10},{9,11},{10,... | collective-permute-start | bytes 1572872 | tf_op jit(solution)/shard_map/ppermute | solution.py:52
  45.4 11.9 %collective-permute-start.14 = (bf16[256,512]{1,0:T(8,128)(2,1)}, bf16[256,512]{1,0:T(8,128)(2,1)}, u32[]{:S(2)}, u32[]{:S(2)}) collective-permute-start(bf16[256,512]{1,0:T(8,128)(2,1)} %collective-permute-done.9.refs_2_), channel_id=1, source_target_pairs={{0,4},{1,5},{2,6},{3,7},{4,8},{5,9},{6,10},{7,11},{8,12},{9,13},{1... | collective-permute-start | bytes 786440 | tf_op jit(solution)/shard_map/ppermute | solution.py:52
  45.4 11.9 %collective-permute-start.15 = (bf16[256,512]{1,0:T(8,128)(2,1)}, bf16[256,512]{1,0:T(8,128)(2,1)}, u32[]{:S(2)}, u32[]{:S(2)}) collective-permute-start(bf16[256,512]{1,0:T(8,128)(2,1)} %collective-permute-done.2.refs_3_), channel_id=1, source_target_pairs={{0,28},{1,29},{2,30},{3,31},{4,0},{5,1},{6,2},{7,3},{8,4},{9,5},{1... | collective-permute-start | bytes 786440 | tf_op jit(solution)/shard_map/ppermute | solution.py:52
  57.3 15.5 %collective-permute-start.19 = (bf16[512,512]{1,0:T(8,128)(2,1)}, bf16[512,512]{1,0:T(8,128)(2,1)S(1)}, u32[]{:S(2)}, u32[]{:S(2)}) collective-permute-start(bf16[512,512]{1,0:T(8,128)(2,1)} %get-tuple-element.85), channel_id=1, source_target_pairs={{0,2},{1,3},{2,0},{3,1},{4,6},{5,7},{6,4},{7,5},{8,10},{9,11},{10,... | collective-permute-start | bytes 1572872 | tf_op jit(solution)/shard_map/ppermute | solution.py:52
  60.2 10.7 %collective-permute-start.12 = (bf16[256,512]{1,0:T(8,128)(2,1)}, bf16[256,512]{1,0:T(8,128)(2,1)}, u32[]{:S(2)}, u32[]{:S(2)}) collective-permute-start(bf16[256,512]{1,0:T(8,128)(2,1)} %get-tuple-element.73), channel_id=1, source_target_pairs={{0,4},{1,5},{2,6},{3,7},{4,8},{5,9},{6,10},{7,11},{8,12},{9,13},{1... | collective-permute-start | bytes 786440 | tf_op jit(solution)/shard_map/ppermute | solution.py:52
  60.2 10.7 %collective-permute-start.13 = (bf16[256,512]{1,0:T(8,128)(2,1)}, bf16[256,512]{1,0:T(8,128)(2,1)}, u32[]{:S(2)}, u32[]{:S(2)}) collective-permute-start(bf16[256,512]{1,0:T(8,128)(2,1)} %get-tuple-element.74), channel_id=1, source_target_pairs={{0,28},{1,29},{2,30},{3,31},{4,0},{5,1},{6,2},{7,3},{8,4},{9,5},{1... | collective-permute-start | bytes 786440 | tf_op jit(solution)/shard_map/ppermute | solution.py:52
  62.8 10.0 %collective-permute-start.17 = (bf16[256,512]{1,0:T(8,128)(2,1)}, bf16[256,512]{1,0:T(8,128)(2,1)}, u32[]{:S(2)}, u32[]{:S(2)}) collective-permute-start(bf16[256,512]{1,0:T(8,128)(2,1)} %collective-permute-done.14.refs_3_), channel_id=1, source_target_pairs={{0,4},{1,5},{2,6},{3,7},{4,8},{5,9},{6,10},{7,11},{8,12},{9,13},{1... | collective-permute-start | bytes 786440 | tf_op jit(solution)/shard_map/ppermute | solution.py:52
  62.8 10.0 %collective-permute-start.18 = (bf16[256,512]{1,0:T(8,128)(2,1)}, bf16[256,512]{1,0:T(8,128)(2,1)}, u32[]{:S(2)}, u32[]{:S(2)}) collective-permute-start(bf16[256,512]{1,0:T(8,128)(2,1)} %collective-permute-done.15.refs_2_), channel_id=1, source_target_pairs={{0,28},{1,29},{2,30},{3,31},{4,0},{5,1},{6,2},{7,3},{8,4},{9,5},{1... | collective-permute-start | bytes 786440 | tf_op jit(solution)/shard_map/ppermute | solution.py:52
  72.9 15.0 %collective-permute-start.20 = (bf16[256,1024]{1,0:T(8,128)(2,1)}, bf16[256,1024]{1,0:T(8,128)(2,1)S(1)}, u32[]{:S(2)}, u32[]{:S(2)}) collective-permute-start(bf16[256,1024]{1,0:T(8,128)(2,1)} %add_convert_fusion.1), channel_id=1, source_target_pairs={{0,96},{32,64},{64,32},{96,0},{128,224},{160,192},{192,160},{224,1... | collective-permute-start | bytes 1572872 | tf_op jit(solution)/shard_map/ppermute | solution.py:488
  75.4 7.1 %collective-permute-start.23 = (bf16[256,512]{1,0:T(8,128)(2,1)}, bf16[256,512]{1,0:T(8,128)(2,1)S(1)}, u32[]{:S(2)}, u32[]{:S(2)}) collective-permute-start(bf16[256,512]{1,0:T(8,128)(2,1)} %collective-permute-done.12.refs_6_), channel_id=1, source_target_pairs={{0,2},{1,3},{2,0},{3,1},{4,6},{5,7},{6,4},{7,5},{8,10},{9,11},{10,... | collective-permute-start | bytes 786440 | tf_op jit(solution)/shard_map/ppermute | solution.py:52
  83.4 7.3 %collective-permute-start.24 = (f32[256,512]{1,0:T(8,128)S(1)}, f32[256,512]{1,0:T(8,128)S(1)}, u32[]{:S(2)}, u32[]{:S(2)}) collective-permute-start(f32[256,512]{1,0:T(8,128)S(1)} %get-tuple-element.98), channel_id=1, source_target_pairs={{0,1},{1,0},{2,3},{3,2},{4,5},{5,4},{6,7},{7,6},{8,9},{9,8},{10,11... | collective-permute-start | bytes 1572872 | tf_op jit(solution)/shard_map/ppermute | solution.py:52
  88.0 12.7 %collective-permute-start.26 = (bf16[256,1024]{1,0:T(8,128)(2,1)S(1)}, bf16[256,1024]{1,0:T(8,128)(2,1)S(1)}, u32[]{:S(2)}, u32[]{:S(2)}) collective-permute-start(bf16[256,1024]{1,0:T(8,128)(2,1)S(1)} %add_convert_fusion), channel_id=1, source_target_pairs={{0,128},{32,160},{64,192},{96,224},{128,0},{160,32},{192,64},{224,... | collective-permute-start | bytes 1572872 | tf_op jit(solution)/shard_map/ppermute | solution.py:506
  (15 other events, 148.3 us)
